TPU v7x, 32 devices: a whole 2x2x4 slice. The times are simulated.
32 devices in a mesh: tile: 8 (over y, x, core), layer: 4 (over z).
Axes of the slice: x: 2, y: 2, z: 4, core: 2. Of those that a mesh axis runs over, the one named last changes fastest.
Arguments:
- classes: int32 [128, 32, 512], P('tile', 'layer'), may hold values from 0 to 15
- well_mask: int32 [128, 32, 512], P('tile', 'layer'), may hold values 0 or 1
- source: float32 [128, 32, 512], P('tile', 'layer'), may hold values from -96 to 96
Outputs:
- pressure: float32 [128, 32, 512], P('tile', 'layer')
Inputs may be any that keep to these rules, and one draw needn't show every extreme that they name: `classes`: an index into the table of 16 permeabilities. `well_mask`: 1 marks a well cell.
All inputs are finite; a program needn't handle non-finite values. No bound on the sum of `well_mask` on one device may be relied on, other than what follows from the above.
Results may differ from a plain program's by a relative error of at most 0.0003.
Values sent between devices are 32-bit elements; how exact they have to be, the bound alone decides.
A program may use at most 64 MiB of HBM per device.

v0:
```python
import jax
import jax.numpy as jnp
import numpy as np
from jax import lax
from jax.sharding import PartitionSpec as P

EDGE = 16
CLASSES = 16
SWEEPS = 4


FINE_DAMPING = 0.67
COARSE_DAMPING = 0.5
SINK_RATE = 0.5
VERTICAL_RATIO = 0.25


def extended(array, sides, width):
    for axis, dim in sides:
        count, length = (lax.axis_size(axis), array.shape[dim])
        up = [(i, (i + 1) % count) for i in range(count - 1)]
        down = [(j, i) for i, j in up]
        last = lax.slice_in_dim(array, length - width, length, axis=dim)
        first = lax.slice_in_dim(array, 0, width, axis=dim)
        before = lax.ppermute(last, axis, up)
        after = lax.ppermute(first, axis, down)
        array = jnp.concatenate([before, array, after], axis=dim)
    return array


def oriented(vector, dimension):
    shape_list = [1, 1, 1]
    shape_list[dimension] = vector.shape[0]
    return vector.reshape(shape_list)


def permeability_of(classes):
    table_values = np.exp(np.linspace(-2.5, 2.5, CLASSES))
    result = jnp.zeros(classes.shape, jnp.float32)
    for entry_index in range(CLASSES):
        result = result + jnp.where(
            classes == entry_index, jnp.float32(table_values[entry_index]), jnp.float32(0.0)
        )
    return result


def harmonic(left_value, right_value):
    summed = left_value + right_value
    safe_sum = jnp.where(summed > 0, summed, 1.0)
    return 2.0 * left_value * right_value / safe_sum


def neighbour(values, dimension, offset):
    starts = [1, 1, 1]
    limits = [values.shape[0] - 1, values.shape[1] - 1, values.shape[2] - 1]
    starts[dimension] += offset
    limits[dimension] += offset
    return lax.slice(values, starts, limits)


def inner_part(values):
    return values[1:-1, 1:-1, 1:-1]


def face_trans(permeability):
    center = inner_part(permeability)
    face_pairs = []
    for dimension in range(3):
        factor = VERTICAL_RATIO if dimension == 1 else 1.0
        lower_trans = factor * harmonic(center, neighbour(permeability, dimension, -1))
        upper_trans = factor * harmonic(center, neighbour(permeability, dimension, 1))
        face_pairs.append((lower_trans, upper_trans))
    return face_pairs


def face_masks(coords, dimension):
    local_index = coords[dimension] % EDGE
    lower_mask = oriented((local_index == 0).astype(jnp.float32), dimension)
    upper_mask = oriented((local_index == EDGE - 1).astype(jnp.float32), dimension)
    return (lower_mask, upper_mask)


def smoothed_basis(permeability, sink_padded, coords):
    face_pairs = face_trans(permeability)
    inside = inner_part(permeability) > 0
    sink_term = inner_part(sink_padded)
    diagonal = sink_term
    for face_pair in face_pairs:
        diagonal = diagonal + face_pair[0] + face_pair[1]
    diagonal = jnp.where(inside, diagonal, 1.0)
    leaving = sink_term
    outer_basis = []
    for dimension in range(3):
        lower_mask, upper_mask = face_masks(coords, dimension)
        across = lower_mask * face_pairs[dimension][0] + upper_mask * face_pairs[dimension][1]
        leaving = leaving + across
        outer_basis.append(jnp.where(inside, FINE_DAMPING * across / diagonal, 0.0))
    own_basis = jnp.where(inside, 1.0 - FINE_DAMPING * leaving / diagonal, 0.0)
    return (own_basis, outer_basis, face_pairs, sink_term)


def colour_probe(own_basis, outer_basis, coords, colour):
    parity = [oriented(coords[dimension] // EDGE % 2, dimension) for dimension in range(3)]
    matches = [
        (parity[dimension] == colour[dimension]).astype(jnp.float32) for dimension in range(3)
    ]
    values = own_basis * matches[0] * matches[1] * matches[2]
    for dimension in range(3):
        weight_mask = 1.0 - matches[dimension]
        for other_dim in range(3):
            if other_dim != dimension:
                weight_mask = weight_mask * matches[other_dim]
        values = values + outer_basis[dimension] * weight_mask
    return values


def apply_operator(values, face_pairs, sink_term):
    center = inner_part(values)
    applied = sink_term * center
    for dimension in range(3):
        applied = applied + face_pairs[dimension][0] * (center - neighbour(values, dimension, -1))
        applied = applied + face_pairs[dimension][1] * (center - neighbour(values, dimension, 1))
    return applied


def half_sum(values):
    size_x, size_z, size_y = values.shape
    half_edge = EDGE // 2
    return values.reshape(
        size_x // half_edge,
        half_edge,
        size_z // half_edge,
        half_edge,
        size_y // half_edge,
        half_edge,
    ).sum(axis=(1, 3, 5))


def routing(halves, row_index, colour_bit, outer_term):
    parent = halves // 2
    sign_value = 2 * (halves % 2) - 1
    if outer_term:
        target = parent + sign_value
        toward = -sign_value
    else:
        target = parent
        toward = sign_value
    offset = jnp.where(target % 2 == colour_bit, 0, toward)
    hit_row = row_index[:, None] == target[None, :]
    return jnp.stack(
        [
            (hit_row & (offset[None, :] == shift_value)).astype(jnp.float32)
            for shift_value in (-1, 0, 1)
        ]
    )


def assemble(
    own_wide,
    outer_wide,
    coords_wide,
    face_pairs,
    sink_term,
    own_basis,
    outer_basis,
    source,
    halves,
    row_index,
):
    row_shape = (row_index[0].shape[0], row_index[1].shape[0], row_index[2].shape[0])
    stiffness = jnp.zeros((3, 3, 3) + row_shape, jnp.float32)
    rhs_sum = jnp.zeros(row_shape, jnp.float32)
    weights = [own_basis] + list(outer_basis)
    for term_index in range(4):
        outer_flags = [term_index == dimension + 1 for dimension in range(3)]
        row_maps = [
            routing(halves[dimension], row_index[dimension], 0, outer_flags[dimension]).sum(axis=0)
            for dimension in range(3)
        ]
        half_sums = half_sum(weights[term_index] * source)
        rhs_sum = rhs_sum + jnp.einsum(
            "ih,jg,kf,hgf->ijk",
            row_maps[0],
            row_maps[1],
            row_maps[2],
            half_sums,
            precision=lax.Precision.HIGHEST,
        )
    for bit_x in (0, 1):
        for bit_z in (0, 1):
            for bit_y in (0, 1):
                colour = (bit_x, bit_z, bit_y)
                applied = apply_operator(
                    colour_probe(own_wide, outer_wide, coords_wide, colour), face_pairs, sink_term
                )
                for term_index in range(4):
                    outer_flags = [term_index == dimension + 1 for dimension in range(3)]
                    route_mats = [
                        routing(
                            halves[dimension],
                            row_index[dimension],
                            colour[dimension],
                            outer_flags[dimension],
                        )
                        for dimension in range(3)
                    ]
                    half_sums = half_sum(weights[term_index] * applied)
                    stiffness = stiffness + jnp.einsum(
                        "aih,bjg,ckf,hgf->abcijk",
                        route_mats[0],
                        route_mats[1],
                        route_mats[2],
                        half_sums,
                        precision=lax.Precision.HIGHEST,
                    )
    return jnp.concatenate([stiffness.reshape((27,) + row_shape), rhs_sum[None]], axis=0)


def coarse_apply(stiffness, padded):
    size_x = padded.shape[0] - 2
    size_z = padded.shape[1] - 2
    size_y = padded.shape[2] - 2
    result = jnp.zeros((size_x, size_z, size_y), jnp.float32)
    for offset_index in range(27):
        step_x = offset_index // 9
        step_z = offset_index // 3 % 3
        step_y = offset_index % 3
        result = (
            result
            + stiffness[offset_index]
            * padded[step_x : step_x + size_x, step_z : step_z + size_z, step_y : step_y + size_y]
        )
    return result


def jacobi_step(coarse_rows, padded, pressure):
    residual = coarse_rows[27] - coarse_apply(coarse_rows[:27], padded)
    return pressure + COARSE_DAMPING * residual / coarse_rows[13]


def expand_coarse(coarse_block, shifts, fine_shape, fine_offsets):
    values = coarse_block
    for dimension in range(3):
        first_row = EDGE * (1 + shifts[dimension]) + fine_offsets[dimension]
        values = lax.dynamic_slice_in_dim(
            jnp.repeat(values, EDGE, axis=dimension), first_row, fine_shape[dimension], dimension
        )
    return values


def prolong(coarse_block, own_basis, outer_basis, coords, fine_shape, fine_offsets):
    result = own_basis * expand_coarse(coarse_block, (0, 0, 0), fine_shape, fine_offsets)
    for dimension in range(3):
        lower_mask, upper_mask = face_masks(coords, dimension)
        minus_shift = [0, 0, 0]
        minus_shift[dimension] = -1
        plus_shift = [0, 0, 0]
        plus_shift[dimension] = 1
        beside = lower_mask * expand_coarse(coarse_block, minus_shift, fine_shape, fine_offsets)
        beside = beside + upper_mask * expand_coarse(
            coarse_block, plus_shift, fine_shape, fine_offsets
        )
        result = result + outer_basis[dimension] * beside
    return result


def ghost_edges(summed):
    return jnp.concatenate([summed[:, :1], summed[:, -1:]], axis=1)


def fold_ghosts(summed, folded):
    own_rows = summed[:, 1:-1]
    own_rows = own_rows.at[:, 0].add(folded[:, 0])
    own_rows = own_rows.at[:, -1].add(folded[:, 3])
    return own_rows


def body(classes, well_mask, source):
    width_x, depth_z, length_y = classes.shape
    layers = lax.axis_size("layer")
    start_x = lax.axis_index("tile") * width_x
    start_z = lax.axis_index("layer") * depth_z
    permeability = permeability_of(classes)
    sink_field = SINK_RATE * well_mask.astype(jnp.float32) * permeability
    stacked = jnp.stack([permeability, sink_field])
    coords_inner = [
        start_x + jnp.arange(width_x, dtype=jnp.int32),
        start_z + jnp.arange(depth_z, dtype=jnp.int32),
        jnp.arange(length_y, dtype=jnp.int32),
    ]
    coords_wide = [
        start_x - 1 + jnp.arange(width_x + 2, dtype=jnp.int32),
        start_z - 1 + jnp.arange(depth_z + 2, dtype=jnp.int32),
        jnp.arange(-1, length_y + 1, dtype=jnp.int32),
    ]
    thin_rim = extended(stacked, (("tile", 1), ("layer", 2)), 1)
    thin_rim = jnp.pad(thin_rim, ((0, 0), (0, 0), (0, 0), (1, 1)))
    own_basis, outer_basis, face_pairs, sink_term = smoothed_basis(
        thin_rim[0], thin_rim[1], coords_inner
    )
    basis_wide = extended(jnp.stack([own_basis] + outer_basis), (("tile", 1), ("layer", 2)), 1)
    basis_wide = jnp.pad(basis_wide, ((0, 0), (0, 0), (0, 0), (1, 1)))
    own_wide = basis_wide[0]
    outer_wide = [basis_wide[1], basis_wide[2], basis_wide[3]]
    half_edge = EDGE // 2
    cells_x = width_x // EDGE
    cells_y = length_y // EDGE
    first_cell = start_x // EDGE
    halves = [
        start_x // half_edge + jnp.arange(width_x // half_edge, dtype=jnp.int32),
        start_z // half_edge + jnp.arange(depth_z // half_edge, dtype=jnp.int32),
        jnp.arange(length_y // half_edge, dtype=jnp.int32),
    ]
    rows_x = first_cell - 1 + jnp.arange(cells_x + 2, dtype=jnp.int32)
    rows_y = jnp.arange(cells_y, dtype=jnp.int32)
    rows_z = jnp.arange(layers * depth_z // EDGE, dtype=jnp.int32)
    partial_rows = assemble(
        own_wide,
        outer_wide,
        coords_wide,
        face_pairs,
        sink_term,
        own_basis,
        outer_basis,
        source,
        halves,
        [rows_x, rows_z, rows_y],
    )
    summed = lax.psum(partial_rows, "layer")
    folded = extended(ghost_edges(summed), (("tile", 1),), 1)
    own_rows = fold_ghosts(summed, folded)

    def column_rim(values):
        return extended(values, (("tile", 0),), 1)

    pressure = jnp.zeros((cells_x, own_rows.shape[2], cells_y), jnp.float32)
    for sweep_index in range(SWEEPS):
        padded = jnp.pad(column_rim(pressure), ((0, 0), (1, 1), (1, 1)))
        pressure = jacobi_step(own_rows, padded, pressure)
    final_pad = jnp.pad(column_rim(pressure), ((0, 0), (1, 1), (1, 1)))
    coarse_block = lax.dynamic_slice_in_dim(final_pad, start_z // EDGE, 3, 1)
    return prolong(
        coarse_block,
        own_basis,
        outer_basis,
        coords_inner,
        (width_x, depth_z, length_y),
        (0, start_z % EDGE, 0),
    )


def solution(mesh):
    in_specs = (P("tile", "layer", None), P("tile", "layer", None), P("tile", "layer", None))
    out_specs = P("tile", "layer", None)
    return jax.shard_map(body, mesh=mesh, in_specs=in_specs, out_specs=out_specs, check_vma=False)
```

profile of v0, /device:TPU:3, one launch (start us, length us, event | category | flops | bytes accessed | tf_op | source)
XLA Modules:
  0.0 170.3 jit_solution(10618926615260727282)
XLA Ops:
  0.6 3.7 %collective-permute-start.10 = (f32[1,2,32]{2,1,0:T(2,128)}, f32[1,2,32]{2,1,0:T(2,128)}, u32[]{:S(2)}, u32[]{:S(2)}) collective-permute-start(f32[1,2,32]{2,1,0:T(2,128)} %broadcast_in_dim.259), channel_id=1, source_target_pairs={{0,4},{4,8},{8,12},{12,16},{16,20},{20,24},{24,28},{1,5},{5,9},{9,... | collective-permute-start | bytes 776 | tf_op jit(solution)/shard_map/ppermute | solution.py:25
  4.2 1.9 %collective-permute-start.11 = (f32[1,2,32]{2,1,0:T(2,128)}, f32[1,2,32]{2,1,0:T(2,128)}, u32[]{:S(2)}, u32[]{:S(2)}) collective-permute-start(f32[1,2,32]{2,1,0:T(2,128)} %broadcast_in_dim.259), channel_id=1, source_target_pairs={{4,0},{8,4},{12,8},{16,12},{20,16},{24,20},{28,24},{5,1},{9,5},{13... | collective-permute-start | bytes 776 | tf_op jit(solution)/shard_map/ppermute | solution.py:26
  6.2 1.5 multiply_bitcast_fusion
  7.7 4.5 %collective-permute-start = (f32[2,1,8,512]{3,2,1,0:T(8,128)S(1)}, f32[2,1,8,512]{3,2,1,0:T(8,128)S(1)}, u32[]{:S(2)}, u32[]{:S(2)}) collective-permute-start(f32[2,1,8,512]{3,2,1,0:T(8,128)S(1)} %get-tuple-element.96), channel_id=1, source_target_pairs={{0,4},{4,8},{8,12},{12,16},{16,20},{20,24},{24,28},{1,5},{5,9},{9,... | collective-permute-start | bytes 98312 | tf_op jit(solution)/shard_map/ppermute | solution.py:25
  12.2 1.9 %collective-permute-start.1 = (f32[2,1,8,512]{3,2,1,0:T(8,128)S(1)}, f32[2,1,8,512]{3,2,1,0:T(8,128)S(1)}, u32[]{:S(2)}, u32[]{:S(2)}) collective-permute-start(f32[2,1,8,512]{3,2,1,0:T(8,128)S(1)} %get-tuple-element.97), channel_id=1, source_target_pairs={{4,0},{8,4},{12,8},{16,12},{20,16},{24,20},{28,24},{5,1},{9,5},{13... | collective-permute-start | bytes 98312 | tf_op jit(solution)/shard_map/ppermute | solution.py:26
  21.2 3.2 %collective-permute-start.2 = (f32[2,18,1,512]{3,2,1,0:T(1,128)S(1)}, f32[2,18,1,512]{3,2,1,0:T(1,128)S(1)}, u32[]{:S(2)}, u32[]{:S(2)}) collective-permute-start(f32[2,18,1,512]{3,2,1,0:T(1,128)S(1)} %get-tuple-element.94), channel_id=1, source_target_pairs={{0,1},{1,2},{2,3},{4,5},{5,6},{6,7},{8,9},{9,10},{10,11},{12,13},{... | collective-permute-start | bytes 221192 | tf_op jit(solution)/shard_map/ppermute | solution.py:25
  26.3 3.9 %collective-permute-done.3 = f32[2,18,1,512]{3,2,1,0:T(1,128)S(1)} collective-permute-done((f32[2,18,1,512]{3,2,1,0:T(1,128)S(1)}, f32[2,18,1,512]{3,2,1,0:T(1,128)S(1)}, u32[]{:S(2)}, u32[]{:S(2)}) %collective-permute-start.3) | collective-permute-done | bytes 73760 | tf_op jit(solution)/shard_map/ppermute | solution.py:26
  32.5 5.3 %collective-permute-start.4 = (f32[4,1,8,512]{3,2,1,0:T(8,128)S(1)}, f32[4,1,8,512]{3,2,1,0:T(8,128)S(1)}, u32[]{:S(2)}, u32[]{:S(2)}) collective-permute-start(f32[4,1,8,512]{3,2,1,0:T(8,128)S(1)} %get-tuple-element.92), channel_id=1, source_target_pairs={{0,4},{4,8},{8,12},{12,16},{16,20},{20,24},{24,28},{1,5},{5,9},{9,... | collective-permute-start | bytes 196616 | tf_op jit(solution)/shard_map/ppermute | solution.py:25
  37.8 1.9 %collective-permute-start.5 = (f32[4,1,8,512]{3,2,1,0:T(8,128)S(1)}, f32[4,1,8,512]{3,2,1,0:T(8,128)S(1)}, u32[]{:S(2)}, u32[]{:S(2)}) collective-permute-start(f32[4,1,8,512]{3,2,1,0:T(8,128)S(1)} %get-tuple-element.93), channel_id=1, source_target_pairs={{4,0},{8,4},{12,8},{16,12},{20,16},{24,20},{28,24},{5,1},{9,5},{13... | collective-permute-start | bytes 196616 | tf_op jit(solution)/shard_map/ppermute | solution.py:26
  39.8 4.5 %collective-permute-done.5 = f32[4,1,8,512]{3,2,1,0:T(8,128)S(1)} collective-permute-done((f32[4,1,8,512]{3,2,1,0:T(8,128)S(1)}, f32[4,1,8,512]{3,2,1,0:T(8,128)S(1)}, u32[]{:S(2)}, u32[]{:S(2)}) %collective-permute-start.5) | collective-permute-done | bytes 65568 | tf_op jit(solution)/shard_map/ppermute | solution.py:26
  45.1 3.9 %collective-permute-start.6 = (f32[4,18,1,512]{3,2,1,0:T(1,128)}, f32[4,18,1,512]{3,2,1,0:T(1,128)}, u32[]{:S(2)}, u32[]{:S(2)}) collective-permute-start(f32[4,18,1,512]{3,2,1,0:T(1,128)} %get-tuple-element.90), channel_id=1, source_target_pairs={{0,1},{1,2},{2,3},{4,5},{5,6},{6,7},{8,9},{9,10},{10,11},{12,13},{... | collective-permute-start | bytes 442376 | tf_op jit(solution)/shard_map/ppermute | solution.py:25
  49.0 1.5 collective-permute-start.7
  55.2 1.4 pad_maximum_fusion
  56.7 4.2 %multiply_add_fusion.2 = (f32[18,10,514]{2,1,0:T(8,128)S(1)}, f32[18,10,514]{2,1,0:T(8,128)S(1)}, f32[18,10,514]{2,1,0:T(8,128)S(1)}, f32[18,10,514]{2,1,0:T(8,128)S(1)}) fusion(f32[18,514]{1,0:T(8,128)S(1)} %copy-done.3, f32[18,10]{1,0:T(8,128)} %get-tuple-element.154, f32[18,10]{1,0:T(8,128)} %get-tuple-element.150, f32[18]{0:T(128)} %copy-done.58, ...), kind=kLoop, calls=%fused_computation.61 | loop fusion | flops 4440960 | bytes 3036040 | tf_op jit(solution)/shard_map/add | solution.py:113
  61.1 3.4 %multiply_add_fusion.4 = (f32[18,10,514]{2,1,0:T(8,128)S(1)}, f32[18,10,514]{2,1,0:T(8,128)S(1)}, f32[18,10,514]{2,1,0:T(8,128)S(1)}, f32[18,10,514]{2,1,0:T(8,128)S(1)}) fusion(f32[18,10]{1,0:T(8,128)S(1)} %get-tuple-element.152, f32[18,10]{1,0:T(8,128)S(1)} %copy-done.35, f32[10]{0:T(128)S(1)} %copy-done.55, f32[18,514]{1,0:T(8,128)S(1)} %copy-done.1, ...), kind=kLoop, calls=%fused_computation.63 | loop fusion | flops 4440960 | bytes 3036040 | tf_op jit(solution)/shard_map/add | solution.py:113
  64.5 7.3 %multiply_reduce_fusion.33 = (f32[16,512]{1,0:T(8,128)}, f32[16,512]{1,0:T(8,128)}, f32[16,512]{1,0:T(8,128)S(1)}, f32[16,512]{1,0:T(8,128)S(1)}, f32[16,512]{1,...) fusion(f32[16,8,512]{2,1,0:T(8,128)S(1)} %get-tuple-element.99,, ...), kind=kLoop, calls=%fused_computation.251 | loop fusion | flops 14516224 | bytes 19005440 | tf_op jit(solution)/shard_map/reduce_sum | solution.py:136
  107.2 16.4 %psum.7 = f32[28,3,2,32]{3,2,1,0:T(2,128)S(1)} all-reduce(f32[28,3,2,32]{3,2,1,0:T(2,128)S(1)} %pad_maximum_fusion.7), channel_id=1, replica_groups=mesh['tile'=8,'layer'=4] {'layer'}, use_global_device_ids=true, to_apply=%region_72.73 | all-reduce | flops 5376 | bytes 43008 | tf_op jit(solution)/shard_map/psum | solution.py:329
  123.7 5.6 %collective-permute-start.8 = (f32[28,1,2,32]{3,2,1,0:T(2,128)S(1)}, f32[28,1,2,32]{3,2,1,0:T(2,128)S(1)}, u32[]{:S(2)}, u32[]{:S(2)}) collective-permute-start(f32[28,1,2,32]{3,2,1,0:T(2,128)S(1)} %get-tuple-element.101), channel_id=1, source_target_pairs={{0,4},{4,8},{8,12},{12,16},{16,20},{20,24},{24,28},{1,5},{5,9},{9,... | collective-permute-start | bytes 21512 | tf_op jit(solution)/shard_map/ppermute | solution.py:25
  129.3 1.9 %collective-permute-start.9 = (f32[28,1,2,32]{3,2,1,0:T(2,128)S(1)}, f32[28,1,2,32]{3,2,1,0:T(2,128)S(1)}, u32[]{:S(2)}, u32[]{:S(2)}) collective-permute-start(f32[28,1,2,32]{3,2,1,0:T(2,128)S(1)} %get-tuple-element.102), channel_id=1, source_target_pairs={{4,0},{8,4},{12,8},{16,12},{20,16},{24,20},{28,24},{5,1},{9,5},{13... | collective-permute-start | bytes 21512 | tf_op jit(solution)/shard_map/ppermute | solution.py:26
  132.0 3.4 %collective-permute-done.9 = f32[28,1,2,32]{3,2,1,0:T(2,128)S(1)} collective-permute-done((f32[28,1,2,32]{3,2,1,0:T(2,128)S(1)}, f32[28,1,2,32]{3,2,1,0:T(2,128)S(1)}, u32[]{:S(2)}, u32[]{:S(2)}) %collective-permute-start.9) | collective-permute-done | bytes 7200 | tf_op jit(solution)/shard_map/ppermute | solution.py:26
  136.2 1.9 %collective-permute-start.12 = (f32[1,2,32]{2,1,0:T(2,128)S(1)}, f32[1,2,32]{2,1,0:T(2,128)S(1)}, u32[]{:S(2)}, u32[]{:S(2)}) collective-permute-start(f32[1,2,32]{2,1,0:T(2,128)S(1)} %fusion.318), channel_id=1, source_target_pairs={{0,4},{4,8},{8,12},{12,16},{16,20},{20,24},{24,28},{1,5},{5,9},{9,... | collective-permute-start | bytes 776 | tf_op jit(solution)/shard_map/ppermute | solution.py:25
  138.2 2.4 %collective-permute-start.13 = (f32[1,2,32]{2,1,0:T(2,128)S(1)}, f32[1,2,32]{2,1,0:T(2,128)S(1)}, u32[]{:S(2)}, u32[]{:S(2)}) collective-permute-start(f32[1,2,32]{2,1,0:T(2,128)S(1)} %fusion.318), channel_id=1, source_target_pairs={{4,0},{8,4},{12,8},{16,12},{20,16},{24,20},{28,24},{5,1},{9,5},{13... | collective-permute-start | bytes 776 | tf_op jit(solution)/shard_map/ppermute | solution.py:26
  140.6 3.4 %collective-permute-done.13 = f32[1,2,32]{2,1,0:T(2,128)S(1)} collective-permute-done((f32[1,2,32]{2,1,0:T(2,128)S(1)}, f32[1,2,32]{2,1,0:T(2,128)S(1)}, u32[]{:S(2)}, u32[]{:S(2)}) %collective-permute-start.13) | collective-permute-done | bytes 288 | tf_op jit(solution)/shard_map/ppermute | solution.py:26
  144.1 2.0 %collective-permute-start.14 = (f32[1,2,32]{2,1,0:T(2,128)S(1)}, f32[1,2,32]{2,1,0:T(2,128)S(1)}, u32[]{:S(2)}, u32[]{:S(2)}) collective-permute-start(f32[1,2,32]{2,1,0:T(2,128)S(1)} %fusion.378), channel_id=1, source_target_pairs={{0,4},{4,8},{8,12},{12,16},{16,20},{20,24},{24,28},{1,5},{5,9},{9,... | collective-permute-start | bytes 776 | tf_op jit(solution)/shard_map/ppermute | solution.py:25
  146.1 2.4 %collective-permute-start.15 = (f32[1,2,32]{2,1,0:T(2,128)S(1)}, f32[1,2,32]{2,1,0:T(2,128)S(1)}, u32[]{:S(2)}, u32[]{:S(2)}) collective-permute-start(f32[1,2,32]{2,1,0:T(2,128)S(1)} %fusion.378), channel_id=1, source_target_pairs={{4,0},{8,4},{12,8},{16,12},{20,16},{24,20},{28,24},{5,1},{9,5},{13... | collective-permute-start | bytes 776 | tf_op jit(solution)/shard_map/ppermute | solution.py:26
  148.5 3.4 %collective-permute-done.15 = f32[1,2,32]{2,1,0:T(2,128)S(1)} collective-permute-done((f32[1,2,32]{2,1,0:T(2,128)S(1)}, f32[1,2,32]{2,1,0:T(2,128)S(1)}, u32[]{:S(2)}, u32[]{:S(2)}) %collective-permute-start.15) | collective-permute-done | bytes 288 | tf_op jit(solution)/shard_map/ppermute | solution.py:26
  152.1 2.0 %collective-permute-start.16 = (f32[1,2,32]{2,1,0:T(2,128)S(1)}, f32[1,2,32]{2,1,0:T(2,128)S(1)}, u32[]{:S(2)}, u32[]{:S(2)}) collective-permute-start(f32[1,2,32]{2,1,0:T(2,128)S(1)} %fusion.377), channel_id=1, source_target_pairs={{0,4},{4,8},{8,12},{12,16},{16,20},{20,24},{24,28},{1,5},{5,9},{9,... | collective-permute-start | bytes 776 | tf_op jit(solution)/shard_map/ppermute | solution.py:25
  154.0 2.4 %collective-permute-start.17 = (f32[1,2,32]{2,1,0:T(2,128)S(1)}, f32[1,2,32]{2,1,0:T(2,128)S(1)}, u32[]{:S(2)}, u32[]{:S(2)}) collective-permute-start(f32[1,2,32]{2,1,0:T(2,128)S(1)} %fusion.377), channel_id=1, source_target_pairs={{4,0},{8,4},{12,8},{16,12},{20,16},{24,20},{28,24},{5,1},{9,5},{13... | collective-permute-start | bytes 776 | tf_op jit(solution)/shard_map/ppermute | solution.py:26
  156.4 3.4 %collective-permute-done.17 = f32[1,2,32]{2,1,0:T(2,128)S(1)} collective-permute-done((f32[1,2,32]{2,1,0:T(2,128)S(1)}, f32[1,2,32]{2,1,0:T(2,128)S(1)}, u32[]{:S(2)}, u32[]{:S(2)}) %collective-permute-start.17) | collective-permute-done | bytes 288 | tf_op jit(solution)/shard_map/ppermute | solution.py:26
  160.0 2.0 %collective-permute-start.18 = (f32[1,2,32]{2,1,0:T(2,128)S(1)}, f32[1,2,32]{2,1,0:T(2,128)S(1)}, u32[]{:S(2)}, u32[]{:S(2)}) collective-permute-start(f32[1,2,32]{2,1,0:T(2,128)S(1)} %fusion.376), channel_id=1, source_target_pairs={{0,4},{4,8},{8,12},{12,16},{16,20},{20,24},{24,28},{1,5},{5,9},{9,... | collective-permute-start | bytes 776 | tf_op jit(solution)/shard_map/ppermute | solution.py:25
  162.0 2.4 %collective-permute-start.19 = (f32[1,2,32]{2,1,0:T(2,128)S(1)}, f32[1,2,32]{2,1,0:T(2,128)S(1)}, u32[]{:S(2)}, u32[]{:S(2)}) collective-permute-start(f32[1,2,32]{2,1,0:T(2,128)S(1)} %fusion.376), channel_id=1, source_target_pairs={{4,0},{8,4},{12,8},{16,12},{20,16},{24,20},{28,24},{5,1},{9,5},{13... | collective-permute-start | bytes 776 | tf_op jit(solution)/shard_map/ppermute | solution.py:26
  164.4 3.4 %collective-permute-done.19 = f32[1,2,32]{2,1,0:T(2,128)S(1)} collective-permute-done((f32[1,2,32]{2,1,0:T(2,128)S(1)}, f32[1,2,32]{2,1,0:T(2,128)S(1)}, u32[]{:S(2)}, u32[]{:S(2)}) %collective-permute-start.19) | collective-permute-done | bytes 288 | tf_op jit(solution)/shard_map/ppermute | solution.py:26
  (473 shorter events, 55.2 us)
Async XLA Ops:
  0.6 130.7 %collective-permute-start.10 = (f32[1,2,32]{2,1,0:T(2,128)}, f32[1,2,32]{2,1,0:T(2,128)}, u32[]{:S(2)}, u32[]{:S(2)}) collective-permute-start(f32[1,2,32]{2,1,0:T(2,128)} %broadcast_in_dim.259), channel_id=1, source_target_pairs={{0,4},{4,8},{8,12},{12,16},{16,20},{20,24},{24,28},{1,5},{5,9},{9,... | collective-permute-start | bytes 776 | tf_op jit(solution)/shard_map/ppermute | solution.py:25
  4.2 127.0 %collective-permute-start.11 = (f32[1,2,32]{2,1,0:T(2,128)}, f32[1,2,32]{2,1,0:T(2,128)}, u32[]{:S(2)}, u32[]{:S(2)}) collective-permute-start(f32[1,2,32]{2,1,0:T(2,128)} %broadcast_in_dim.259), channel_id=1, source_target_pairs={{4,0},{8,4},{12,8},{16,12},{20,16},{24,20},{28,24},{5,1},{9,5},{13... | collective-permute-start | bytes 776 | tf_op jit(solution)/shard_map/ppermute | solution.py:26
  7.7 13.4 %collective-permute-start = (f32[2,1,8,512]{3,2,1,0:T(8,128)S(1)}, f32[2,1,8,512]{3,2,1,0:T(8,128)S(1)}, u32[]{:S(2)}, u32[]{:S(2)}) collective-permute-start(f32[2,1,8,512]{3,2,1,0:T(8,128)S(1)} %get-tuple-element.96), channel_id=1, source_target_pairs={{0,4},{4,8},{8,12},{12,16},{16,20},{20,24},{24,28},{1,5},{5,9},{9,... | collective-permute-start | bytes 98312 | tf_op jit(solution)/shard_map/ppermute | solution.py:25
  12.2 8.8 %collective-permute-start.1 = (f32[2,1,8,512]{3,2,1,0:T(8,128)S(1)}, f32[2,1,8,512]{3,2,1,0:T(8,128)S(1)}, u32[]{:S(2)}, u32[]{:S(2)}) collective-permute-start(f32[2,1,8,512]{3,2,1,0:T(8,128)S(1)} %get-tuple-element.97), channel_id=1, source_target_pairs={{4,0},{8,4},{12,8},{16,12},{20,16},{24,20},{28,24},{5,1},{9,5},{13... | collective-permute-start | bytes 98312 | tf_op jit(solution)/shard_map/ppermute | solution.py:26
  14.1 18.0 %copy-start.38 = (f32[512]{0:T(512)}, f32[512]{0:T(512)S(1)}, u32[]{:S(2)}) copy-start(f32[512]{0:T(512)S(1)} %get-tuple-element.160) | copy-start | bytes 6148
  14.2 18.0 %copy-start.40 = (f32[512]{0:T(512)}, f32[512]{0:T(512)S(1)}, u32[]{:S(2)}) copy-start(f32[512]{0:T(512)S(1)} %get-tuple-element.161) | copy-start | bytes 6148
  14.2 18.0 %copy-start.48 = (f32[16]{0:T(128)}, f32[16]{0:T(128)S(1)}, u32[]{:S(2)}) copy-start(f32[16]{0:T(128)S(1)} %get-tuple-element.170) | copy-start | bytes 196
  14.2 18.0 %copy-start.50 = (f32[16]{0:T(128)}, f32[16]{0:T(128)S(1)}, u32[]{:S(2)}) copy-start(f32[16]{0:T(128)S(1)} %get-tuple-element.171) | copy-start | bytes 196
  21.2 5.1 %collective-permute-start.2 = (f32[2,18,1,512]{3,2,1,0:T(1,128)S(1)}, f32[2,18,1,512]{3,2,1,0:T(1,128)S(1)}, u32[]{:S(2)}, u32[]{:S(2)}) collective-permute-start(f32[2,18,1,512]{3,2,1,0:T(1,128)S(1)} %get-tuple-element.94), channel_id=1, source_target_pairs={{0,1},{1,2},{2,3},{4,5},{5,6},{6,7},{8,9},{9,10},{10,11},{12,13},{... | collective-permute-start | bytes 221192 | tf_op jit(solution)/shard_map/ppermute | solution.py:25
  24.5 5.8 %collective-permute-start.3 = (f32[2,18,1,512]{3,2,1,0:T(1,128)S(1)}, f32[2,18,1,512]{3,2,1,0:T(1,128)S(1)}, u32[]{:S(2)}, u32[]{:S(2)}) collective-permute-start(f32[2,18,1,512]{3,2,1,0:T(1,128)S(1)} %get-tuple-element.95), channel_id=1, source_target_pairs={{1,0},{2,1},{3,2},{5,4},{6,5},{7,6},{9,8},{10,9},{11,10},{13,12},{... | collective-permute-start | bytes 221192 | tf_op jit(solution)/shard_map/ppermute | solution.py:26
  32.5 7.3 %collective-permute-start.4 = (f32[4,1,8,512]{3,2,1,0:T(8,128)S(1)}, f32[4,1,8,512]{3,2,1,0:T(8,128)S(1)}, u32[]{:S(2)}, u32[]{:S(2)}) collective-permute-start(f32[4,1,8,512]{3,2,1,0:T(8,128)S(1)} %get-tuple-element.92), channel_id=1, source_target_pairs={{0,4},{4,8},{8,12},{12,16},{16,20},{20,24},{24,28},{1,5},{5,9},{9,... | collective-permute-start | bytes 196616 | tf_op jit(solution)/shard_map/ppermute | solution.py:25
  37.8 6.5 %collective-permute-start.5 = (f32[4,1,8,512]{3,2,1,0:T(8,128)S(1)}, f32[4,1,8,512]{3,2,1,0:T(8,128)S(1)}, u32[]{:S(2)}, u32[]{:S(2)}) collective-permute-start(f32[4,1,8,512]{3,2,1,0:T(8,128)S(1)} %get-tuple-element.93), channel_id=1, source_target_pairs={{4,0},{8,4},{12,8},{16,12},{20,16},{24,20},{28,24},{5,1},{9,5},{13... | collective-permute-start | bytes 196616 | tf_op jit(solution)/shard_map/ppermute | solution.py:26
  45.1 10.0 %collective-permute-start.6 = (f32[4,18,1,512]{3,2,1,0:T(1,128)}, f32[4,18,1,512]{3,2,1,0:T(1,128)}, u32[]{:S(2)}, u32[]{:S(2)}) collective-permute-start(f32[4,18,1,512]{3,2,1,0:T(1,128)} %get-tuple-element.90), channel_id=1, source_target_pairs={{0,1},{1,2},{2,3},{4,5},{5,6},{6,7},{8,9},{9,10},{10,11},{12,13},{... | collective-permute-start | bytes 442376 | tf_op jit(solution)/shard_map/ppermute | solution.py:25
  49.0 6.2 %collective-permute-start.7 = (f32[4,18,1,512]{3,2,1,0:T(1,128)}, f32[4,18,1,512]{3,2,1,0:T(1,128)}, u32[]{:S(2)}, u32[]{:S(2)}) collective-permute-start(f32[4,18,1,512]{3,2,1,0:T(1,128)} %get-tuple-element.91), channel_id=1, source_target_pairs={{1,0},{2,1},{3,2},{5,4},{6,5},{7,6},{9,8},{10,9},{11,10},{13,12},{... | collective-permute-start | bytes 442376 | tf_op jit(solution)/shard_map/ppermute | solution.py:26
  103.5 64.3 %copy-start.46 = (pred[3,4,34]{2,1,0:T(4,128)(4,1)S(1)}, pred[3,4,34]{2,1,0:T(4,128)(4,1)}, u32[]{:S(2)}) copy-start(pred[3,4,34]{2,1,0:T(4,128)(4,1)} %get-tuple-element.218) | copy-start | bytes 1228
  103.5 64.3 %copy-start.47 = (pred[3,4,34]{2,1,0:T(4,128)(4,1)S(1)}, pred[3,4,34]{2,1,0:T(4,128)(4,1)}, u32[]{:S(2)}) copy-start(pred[3,4,34]{2,1,0:T(4,128)(4,1)} %get-tuple-element.219) | copy-start | bytes 1228
  105.2 64.1 %copy-start.39 = (f32[512]{0:T(512)S(1)}, f32[512]{0:T(512)}, u32[]{:S(2)}) copy-start(f32[512]{0:T(512)} %copy-done.38) | copy-start | bytes 6148
  105.2 64.1 %copy-start.41 = (f32[512]{0:T(512)S(1)}, f32[512]{0:T(512)}, u32[]{:S(2)}) copy-start(f32[512]{0:T(512)} %copy-done.40) | copy-start | bytes 6148
  105.2 64.1 %copy-start.49 = (f32[16]{0:T(128)S(1)}, f32[16]{0:T(128)}, u32[]{:S(2)}) copy-start(f32[16]{0:T(128)} %copy-done.48) | copy-start | bytes 196
  105.2 64.1 %copy-start.51 = (f32[16]{0:T(128)S(1)}, f32[16]{0:T(128)}, u32[]{:S(2)}) copy-start(f32[16]{0:T(128)} %copy-done.50) | copy-start | bytes 196
  105.2 64.1 %copy-start.61 = (f32[8]{0:T(128)S(1)}, f32[8]{0:T(128)}, u32[]{:S(2)}) copy-start(f32[8]{0:T(128)} %get-tuple-element.172) | copy-start | bytes 100
  105.3 64.1 %copy-start.62 = (f32[8]{0:T(128)S(1)}, f32[8]{0:T(128)}, u32[]{:S(2)}) copy-start(f32[8]{0:T(128)} %get-tuple-element.173) | copy-start | bytes 100
  123.7 8.4 %collective-permute-start.8 = (f32[28,1,2,32]{3,2,1,0:T(2,128)S(1)}, f32[28,1,2,32]{3,2,1,0:T(2,128)S(1)}, u32[]{:S(2)}, u32[]{:S(2)}) collective-permute-start(f32[28,1,2,32]{3,2,1,0:T(2,128)S(1)} %get-tuple-element.101), channel_id=1, source_target_pairs={{0,4},{4,8},{8,12},{12,16},{16,20},{20,24},{24,28},{1,5},{5,9},{9,... | collective-permute-start | bytes 21512 | tf_op jit(solution)/shard_map/ppermute | solution.py:25
  129.3 6.1 %collective-permute-start.9 = (f32[28,1,2,32]{3,2,1,0:T(2,128)S(1)}, f32[28,1,2,32]{3,2,1,0:T(2,128)S(1)}, u32[]{:S(2)}, u32[]{:S(2)}) collective-permute-start(f32[28,1,2,32]{3,2,1,0:T(2,128)S(1)} %get-tuple-element.102), channel_id=1, source_target_pairs={{4,0},{8,4},{12,8},{16,12},{20,16},{24,20},{28,24},{5,1},{9,5},{13... | collective-permute-start | bytes 21512 | tf_op jit(solution)/shard_map/ppermute | solution.py:26
  136.2 4.4 %collective-permute-start.12 = (f32[1,2,32]{2,1,0:T(2,128)S(1)}, f32[1,2,32]{2,1,0:T(2,128)S(1)}, u32[]{:S(2)}, u32[]{:S(2)}) collective-permute-start(f32[1,2,32]{2,1,0:T(2,128)S(1)} %fusion.318), channel_id=1, source_target_pairs={{0,4},{4,8},{8,12},{12,16},{16,20},{20,24},{24,28},{1,5},{5,9},{9,... | collective-permute-start | bytes 776 | tf_op jit(solution)/shard_map/ppermute | solution.py:25
  138.2 5.8 %collective-permute-start.13 = (f32[1,2,32]{2,1,0:T(2,128)S(1)}, f32[1,2,32]{2,1,0:T(2,128)S(1)}, u32[]{:S(2)}, u32[]{:S(2)}) collective-permute-start(f32[1,2,32]{2,1,0:T(2,128)S(1)} %fusion.318), channel_id=1, source_target_pairs={{4,0},{8,4},{12,8},{16,12},{20,16},{24,20},{28,24},{5,1},{9,5},{13... | collective-permute-start | bytes 776 | tf_op jit(solution)/shard_map/ppermute | solution.py:26
  144.1 4.3 %collective-permute-start.14 = (f32[1,2,32]{2,1,0:T(2,128)S(1)}, f32[1,2,32]{2,1,0:T(2,128)S(1)}, u32[]{:S(2)}, u32[]{:S(2)}) collective-permute-start(f32[1,2,32]{2,1,0:T(2,128)S(1)} %fusion.378), channel_id=1, source_target_pairs={{0,4},{4,8},{8,12},{12,16},{16,20},{20,24},{24,28},{1,5},{5,9},{9,... | collective-permute-start | bytes 776 | tf_op jit(solution)/shard_map/ppermute | solution.py:25
  146.1 5.8 %collective-permute-start.15 = (f32[1,2,32]{2,1,0:T(2,128)S(1)}, f32[1,2,32]{2,1,0:T(2,128)S(1)}, u32[]{:S(2)}, u32[]{:S(2)}) collective-permute-start(f32[1,2,32]{2,1,0:T(2,128)S(1)} %fusion.378), channel_id=1, source_target_pairs={{4,0},{8,4},{12,8},{16,12},{20,16},{24,20},{28,24},{5,1},{9,5},{13... | collective-permute-start | bytes 776 | tf_op jit(solution)/shard_map/ppermute | solution.py:26
  152.1 4.3 %collective-permute-start.16 = (f32[1,2,32]{2,1,0:T(2,128)S(1)}, f32[1,2,32]{2,1,0:T(2,128)S(1)}, u32[]{:S(2)}, u32[]{:S(2)}) collective-permute-start(f32[1,2,32]{2,1,0:T(2,128)S(1)} %fusion.377), channel_id=1, source_target_pairs={{0,4},{4,8},{8,12},{12,16},{16,20},{20,24},{24,28},{1,5},{5,9},{9,... | collective-permute-start | bytes 776 | tf_op jit(solution)/shard_map/ppermute | solution.py:25
  154.0 5.8 %collective-permute-start.17 = (f32[1,2,32]{2,1,0:T(2,128)S(1)}, f32[1,2,32]{2,1,0:T(2,128)S(1)}, u32[]{:S(2)}, u32[]{:S(2)}) collective-permute-start(f32[1,2,32]{2,1,0:T(2,128)S(1)} %fusion.377), channel_id=1, source_target_pairs={{4,0},{8,4},{12,8},{16,12},{20,16},{24,20},{28,24},{5,1},{9,5},{13... | collective-permute-start | bytes 776 | tf_op jit(solution)/shard_map/ppermute | solution.py:26
  160.0 4.4 %collective-permute-start.18 = (f32[1,2,32]{2,1,0:T(2,128)S(1)}, f32[1,2,32]{2,1,0:T(2,128)S(1)}, u32[]{:S(2)}, u32[]{:S(2)}) collective-permute-start(f32[1,2,32]{2,1,0:T(2,128)S(1)} %fusion.376), channel_id=1, source_target_pairs={{0,4},{4,8},{8,12},{12,16},{16,20},{20,24},{24,28},{1,5},{5,9},{9,... | collective-permute-start | bytes 776 | tf_op jit(solution)/shard_map/ppermute | solution.py:25
  162.0 5.8 %collective-permute-start.19 = (f32[1,2,32]{2,1,0:T(2,128)S(1)}, f32[1,2,32]{2,1,0:T(2,128)S(1)}, u32[]{:S(2)}, u32[]{:S(2)}) collective-permute-start(f32[1,2,32]{2,1,0:T(2,128)S(1)} %fusion.376), channel_id=1, source_target_pairs={{4,0},{8,4},{12,8},{16,12},{20,16},{24,20},{28,24},{5,1},{9,5},{13... | collective-permute-start | bytes 776 | tf_op jit(solution)/shard_map/ppermute | solution.py:26
  (97 other events, 471.8 us)
where the time goes:
time: 171 us; the launch traced here: 170 us
  starting transfers between devices  54 us (32%)
  other arithmetic  37.2 us (22%)
  waiting for transfers between devices  25.9 us (15%)
  local copies, waits for them, and re-layouts  19.6 us (11%)
  blocking collectives  16.4 us (10%)
  matrix products  14.6 us (9%)
  between operations  2.68 us (2%)
    ppermute x10, starting transfers between devices, extended(): before = lax.ppermute(last, axis, up)  34 us
    ppermute x10, waiting for transfers between devices, extended(): after = lax.ppermute(first, axis, down)  25.4 us
    ppermute x10, starting transfers between devices, extended(): after = lax.ppermute(first, axis, down)  19.9 us
    psum x1, blocking collectives, body(): summed = lax.psum(partial_rows, 'layer')  16.4 us
    reduce_sum x36, local copies, waits for them, and re-layouts, half_sum(): return values.reshape(size_x // half_edge, half_edge, size_z // half_edge...  13.4 us
    dot_general x64, matrix products, assemble(): jnp.einsum('aih,bjg,ckf,hgf->abcijk', route_mats[0], route_mats[1], route...  13 us
    reduce_sum x37, other arithmetic, half_sum(): return values.reshape(size_x // half_edge, half_edge, size_z // half_edge...  11.7 us
    add x2, other arithmetic, colour_probe(): values = values + outer_basis[dimension] * weight_mask  7.69 us
  transfers between devices with their start and end apart: 20, of which 8 were waited for; matrix products, arithmetic and copies ran while one was open for 39% of the time, Pallas kernels for 0%

commit v1 on v0

v1 whole, which is shorter than its diff:
```python
import functools

import jax
import jax.numpy as jnp
import numpy as np
from jax import lax
from jax.experimental import pallas as pl
from jax.experimental.pallas import tpu as pltpu
from jax.sharding import PartitionSpec as P

EDGE = 16
HALF = EDGE // 2
CLASSES = 16
SWEEPS = 4
FINE_DAMPING = 0.67
COARSE_DAMPING = 0.5
SINK_RATE = 0.5
VERTICAL_RATIO = 0.25
LANES = 128
SUB = 8
VALUES = 16
RHS = 14
MESH = pl.DeviceIdType.MESH

OWN, OX, OZ, OY = range(4)
FULL_OFFSETS = ((0, 0, 0), (0, 0, 1), (0, 1, 0), (0, 1, 1), None)
EDGE_OFFSETS = ((1, 0, 0), (1, 0, 1), (1, 1, 0))
PRODUCTS = (
    [(w, b, 0) for w in (OWN, OZ, OY) for b in FULL_OFFSETS]
    + [(OX, b, -1) for b in FULL_OFFSETS]
    + [(OX, None, 1)]
    + [(w, b, 1) for w in (OWN, OZ, OY, OX) for b in EDGE_OFFSETS]
    + [(OX, b, -1) for b in EDGE_OFFSETS]
)
SLOT = {product: index for index, product in enumerate(PRODUCTS)}
PADDED = -(-len(PRODUCTS) // SUB) * SUB


def routing_table():
    table = np.zeros((2, 6 * VALUES, 4 * PADDED), np.float32)
    for parity, sign_z in ((0, -1), (1, 1)):
        for n, (weight, toggled, sign_x) in enumerate(PRODUCTS):
            for half, sign_y in ((0, -1), (1, 1)):
                row = ((weight == OX) * sign_x, (weight == OZ) * sign_z, (weight == OY) * sign_y)
                if toggled is None:
                    value = RHS
                else:
                    column = (toggled[0] * sign_x, toggled[1] * sign_z, toggled[2] * sign_y)
                    o = [column[d] - row[d] for d in range(3)]
                    value = 9 * (o[0] + 1) + 3 * (o[1] + 1) + (o[2] + 1) - 13
                    if value < 0:
                        continue
                group = 2 * (weight == OY) + half
                target = (row[0] + 1) * 2 + (weight == OZ)
                table[parity, target * VALUES + value, group * PADDED + n] = 1.0
    return table


def split_dot(table, values, swap=False):
    total = None
    rest = values
    for _ in range(3):
        part = rest.astype(jnp.bfloat16)
        rest = rest - part.astype(jnp.float32)
        pair = (part, table) if swap else (table, part)
        term = jnp.dot(*pair, preferred_element_type=jnp.float32)
        total = term if total is None else total + term
    return total


def harmonic(a, b):
    return 2.0 * a * b / jnp.maximum(a + b, 1e-30)


def perm_of(classes):
    step = 5.0 / (CLASSES - 1)
    return jnp.exp(classes.astype(jnp.float32) * step - 2.5)


def sink_of(well, perm):
    return SINK_RATE * well.astype(jnp.float32) * perm


def kernel(
    tiles, layers, nx, ny,
    cls_hbm, well_hbm, src_hbm, route_hbm, out_ref,
    cls, well, src, route,
    kx, sk, zs, zr, crs, crr,
    typ_s, tzi_s, txf, tzm_s, tzp_s, d_s, own_s, oy_s, oz_s, ox_s, tz_edge, zb,
    zi, acc, part, fold, gsend, gath, gsum, csc,
    in_sem, x_send, x_recv, z_send, z_recv, c_send, c_recv, f_send, f_recv, g_send, g_recv,
):
    tile = lax.axis_index("tile")
    layer = lax.axis_index("layer")
    pairs = layers // 2
    pair = layer // 2
    parity = layer % 2
    cells = ny // EDGE
    span = pairs * cells
    rows = part.shape[1]
    plane = lambda i: pl.ds(i * SUB, SUB)

    loads = [
        pltpu.make_async_copy(a, b, in_sem.at[n])
        for n, (a, b) in enumerate(
            ((cls_hbm, cls), (well_hbm, well), (src_hbm, src), (route_hbm.at[parity], route))
        )
    ]
    for load in loads:
        load.start()

    barrier = pltpu.get_barrier_semaphore()
    me = tile * layers + layer

    def greet(k, carry):
        other = lax.rem(me + k, tiles * layers)
        pl.semaphore_signal(
            barrier, inc=1, device_id=(other // layers, other % layers), device_id_type=MESH
        )
        return carry

    lax.fori_loop(1, tiles * layers, greet, 0)

    loads[0].wait()
    loads[1].wait()

    for i in (0, 1, nx - 2, nx - 1):
        k = perm_of(cls[plane(i), :])
        kx[plane(i + 2), :] = k
        if i in (0, nx - 1):
            sk[plane(i + 1), :] = sink_of(well[plane(i), :], k)
    for side, (z1, z2) in enumerate(((0, 1), (SUB - 1, SUB - 2))):
        for i in range(nx):
            zi[0, pl.ds(i, 1), :] = cls[pl.ds(i * SUB + z1, 1), :]
            zi[1, pl.ds(i, 1), :] = cls[pl.ds(i * SUB + z2, 1), :]
            zi[2, pl.ds(i, 1), :] = well[pl.ds(i * SUB + z1, 1), :]
        k = perm_of(zi[0])
        zs[side, 0] = k
        zs[side, 1] = perm_of(zi[1])
        zs[side, 2] = sink_of(zi[2], k)
        crs[0 + side] = k[0:1, :]
        crs[2 + side] = k[nx - 1 : nx, :]

    pl.semaphore_wait(barrier, tiles * layers - 1)

    def halo_copies(sx):
        lo = sx < 0
        src_k = kx.at[pl.ds((2 if lo else nx) * SUB, 2 * SUB), :]
        dst_k = kx.at[pl.ds((nx + 2 if lo else 0) * SUB, 2 * SUB), :]
        src_s = sk.at[plane(1 if lo else nx), :]
        dst_s = sk.at[plane(nx + 1 if lo else 0), :]
        s = 0 if lo else 1
        return [
            pltpu.make_async_remote_copy(
                a, b, x_send.at[s, n], x_recv.at[s, n],
                device_id=(tile + sx, layer), device_id_type=MESH,
            )
            for n, (a, b) in enumerate(((src_k, dst_k), (src_s, dst_s)))
        ]

    def layer_copy(sz):
        s = 0 if sz < 0 else 1
        return pltpu.make_async_remote_copy(
            zs.at[s], zr.at[1 - s], z_send.at[s], z_recv.at[s],
            device_id=(tile, layer + sz), device_id_type=MESH,
        )

    def corner_copy(sx, sz):
        a, b = (0 if sx < 0 else 1), (0 if sz < 0 else 1)
        return pltpu.make_async_remote_copy(
            crs.at[2 * a + b], crr.at[2 * (1 - a) + (1 - b)],
            c_send.at[2 * a + b], c_recv.at[2 * a + b],
            device_id=(tile + sx, layer + sz), device_id_type=MESH,
        )

    def has(sx, sz):
        ok = None
        for s, at, count in ((sx, tile, tiles), (sz, layer, layers)):
            if s:
                test = at > 0 if s < 0 else at < count - 1
                ok = test if ok is None else ok & test
        return ok

    sides = (-1, 1)
    diagonals = [(sx, sz) for sx in sides for sz in sides]
    for sz in sides:
        @pl.when(has(0, sz))
        def _():
            layer_copy(sz).start()

        @pl.when(jnp.logical_not(has(0, sz)))
        def _():
            zr[0 if sz < 0 else 1] = jnp.zeros(zr.shape[1:], jnp.float32)
    for sx in sides:
        @pl.when(has(sx, 0))
        def _():
            for copy in halo_copies(sx):
                copy.start()

        @pl.when(jnp.logical_not(has(sx, 0)))
        def _():
            first = 0 if sx < 0 else nx + 2
            kx[pl.ds(first * SUB, 2 * SUB), :] = jnp.zeros((2 * SUB, ny), jnp.float32)
            sk[plane(0 if sx < 0 else nx + 1), :] = jnp.zeros((SUB, ny), jnp.float32)
    for sx, sz in diagonals:
        @pl.when(has(sx, sz))
        def _():
            corner_copy(sx, sz).start()

        @pl.when(jnp.logical_not(has(sx, sz)))
        def _():
            crr[2 * (0 if sx < 0 else 1) + (0 if sz < 0 else 1)] = jnp.zeros((1, ny), jnp.float32)

    sub = lax.broadcasted_iota(jnp.int32, (SUB, ny), 0)
    lane = lax.broadcasted_iota(jnp.int32, (SUB, ny), 1)
    even = parity == 0
    cross_ym = lane % EDGE == 0
    cross_yp = lane % EDGE == EDGE - 1
    cross_zm = (sub == 0) & even
    cross_zp = (sub == SUB - 1) & jnp.logical_not(even)

    def up(a, dim):
        return pltpu.roll(a, 1, dim)

    def down(a, dim):
        return pltpu.roll(a, a.shape[dim] - 1, dim)

    def y_face(k):
        at = lax.broadcasted_iota(jnp.int32, k.shape, 1)
        return jnp.where(at == ny - 1, 0.0, harmonic(k, down(k, 1)))

    def only(mask, a):
        return jnp.where(mask, a, 0.0)

    def early(i, carry):
        at = pl.ds(pl.multiple_of(i * SUB, SUB), SUB)
        k = perm_of(cls[at, :])
        kx[pl.ds(pl.multiple_of((i + 2) * SUB, SUB), SUB), :] = k
        sk[pl.ds(pl.multiple_of((i + 1) * SUB, SUB), SUB), :] = sink_of(well[at, :], k)
        return carry

    lax.fori_loop(2, nx - 2, early, 0)
    for i in (1, nx - 2):
        sk[plane(i + 1), :] = sink_of(well[plane(i), :], kx[plane(i + 2), :])

    def faces(i, carry):
        at = pl.ds(pl.multiple_of(i * SUB, SUB), SUB)
        k = kx[pl.ds(pl.multiple_of((i + 2) * SUB, SUB), SUB), :]
        typ_s[at, :] = y_face(k)
        tzi_s[at, :] = VERTICAL_RATIO * harmonic(k, up(k, 0))

        @pl.when(i > 0)
        def _():
            before = kx[pl.ds(pl.multiple_of((i + 1) * SUB, SUB), SUB), :]
            txf[at, :] = harmonic(before, k)

        return carry

    lax.fori_loop(0, nx, faces, 0)

    for sz in sides:
        @pl.when(has(0, sz))
        def _():
            layer_copy(-sz).wait_recv()
    for sx in sides:
        @pl.when(has(sx, 0))
        def _():
            for copy in halo_copies(-sx):
                copy.wait_recv()
    for sx, sz in diagonals:
        @pl.when(has(sx, sz))
        def _():
            corner_copy(-sx, -sz).wait_recv()

    def basis(sink, faces, crossing):
        diagonal = sink
        for pair_of in faces:
            diagonal = diagonal + pair_of[0] + pair_of[1]
        inverse = FINE_DAMPING / jnp.maximum(diagonal, 1e-30)
        leaving = sink
        for term in crossing:
            if term is not None:
                leaving = leaving + term
        outer = [None if term is None else term * inverse for term in crossing]
        return diagonal, 1.0 - leaving * inverse, outer

    for side in (0, 1):
        k0 = kx[plane(2 if side == 0 else nx + 1), :]
        k1 = kx[plane(1 if side == 0 else nx + 2), :]
        k2 = kx[plane(0 if side == 0 else nx + 3), :]
        toward = harmonic(k0, k1)
        txf[plane(0 if side == 0 else nx), :] = toward
        inner = VERTICAL_RATIO * harmonic(k1, up(k1, 0))
        tzm = jnp.where(sub == 0, VERTICAL_RATIO * harmonic(k1, crr[2 * side]), inner)
        tzp = jnp.where(
            sub == SUB - 1, VERTICAL_RATIO * harmonic(k1, crr[2 * side + 1]), down(inner, 0)
        )
        typ = y_face(k1)
        tym = up(typ, 1)
        crossing = (
            toward,
            only(cross_zm, tzm) + only(cross_zp, tzp),
            only(cross_ym, tym) + only(cross_yp, typ),
        )
        _, own, outer = basis(
            sk[plane(0 if side == 0 else nx + 1), :],
            ((toward, harmonic(k1, k2)), (tzm, tzp), (tym, typ)),
            crossing,
        )
        at = plane(0 if side == 0 else nx + 1)
        own_s[at, :] = own
        ox_s[plane(0 if side == 0 else 3), :] = outer[0]
        oz_s[at, :] = outer[1]
        oy_s[at, :] = outer[2]

    wide_row = lax.broadcasted_iota(jnp.int32, (nx, ny), 0)
    wide_lane = lax.broadcasted_iota(jnp.int32, (nx, ny), 1)
    for side in (0, 1):
        k0 = zs[side, 0]
        k1 = zr[side, 0]
        k2 = zr[side, 1]
        toward = VERTICAL_RATIO * harmonic(k0, k1)
        tz_edge[side] = toward
        inner = harmonic(k1, up(k1, 0))
        txm = jnp.where(wide_row == 0, harmonic(k1, crr[side]), inner)
        txp = jnp.where(wide_row == nx - 1, harmonic(k1, crr[2 + side]), down(inner, 0))
        typ = y_face(k1)
        tym = up(typ, 1)
        crosses = even if side == 0 else jnp.logical_not(even)
        crossing = (
            only(wide_row == 0, txm) + only(wide_row == nx - 1, txp),
            toward * crosses.astype(jnp.float32),
            only(wide_lane % EDGE == 0, tym) + only(wide_lane % EDGE == EDGE - 1, typ),
        )
        _, own, outer = basis(
            zr[side, 2],
            ((txm, txp), (toward, VERTICAL_RATIO * harmonic(k1, k2)), (tym, typ)),
            crossing,
        )
        zb[side, OWN] = own
        zb[side, OX] = outer[0]
        zb[side, OZ] = outer[1]
        zb[side, OY] = outer[2]

    def block_basis(i, edge):
        at = pl.ds(pl.multiple_of(i * SUB, SUB), SUB)
        after = pl.ds(pl.multiple_of((i + 1) * SUB, SUB), SUB)
        inner = tzi_s[at, :]
        tzm = jnp.where(sub == 0, tz_edge[0, pl.ds(i, 1), :], inner)
        tzp = jnp.where(sub == SUB - 1, tz_edge[1, pl.ds(i, 1), :], down(inner, 0))
        txm = txf[at, :]
        txp = txf[after, :]
        typ = typ_s[at, :]
        tym = up(typ, 1)
        crossing = (
            None if edge == 0 else (txm if edge < 0 else txp),
            only(cross_zm, tzm) + only(cross_zp, tzp),
            only(cross_ym, tym) + only(cross_yp, typ),
        )
        diagonal, own, outer = basis(
            sk[after, :], ((txm, txp), (tzm, tzp), (tym, typ)), crossing
        )
        tzm_s[at, :] = tzm
        tzp_s[at, :] = tzp
        d_s[at, :] = diagonal
        own_s[after, :] = own
        oz_s[after, :] = outer[1]
        oy_s[after, :] = outer[2]
        if edge:
            ox_s[plane(1 if edge < 0 else 2), :] = outer[0]

    block_basis(0, -1)
    lax.fori_loop(1, nx - 1, lambda i, c: (block_basis(i, 0), c)[1], 0)
    block_basis(nx - 1, 1)

    loads[2].wait()
    loads[3].wait()

    acc[...] = jnp.zeros(acc.shape, jnp.float32)

    def add(product, term):
        at = plane(SLOT[product])
        acc[at, :] = acc[at, :] + term

    def products(i, edge):
        at = pl.ds(pl.multiple_of(i * SUB, SUB), SUB)
        mid = pl.ds(pl.multiple_of((i + 1) * SUB, SUB), SUB)
        after = pl.ds(pl.multiple_of((i + 2) * SUB, SUB), SUB)
        row = pl.ds(i, 1)
        diagonal, tzm, tzp, typ = d_s[at, :], tzm_s[at, :], tzp_s[at, :], typ_s[at, :]
        tym = up(typ, 1)
        txm, txp = txf[at, :], txf[mid, :]
        own, oz, oy = own_s[mid, :], oz_s[mid, :], oy_s[mid, :]
        source = src[at, :]

        def z_before(a, kind):
            return jnp.where(sub == 0, zb[0, kind, row, :], up(a, 0))

        def z_after(a, kind):
            return jnp.where(sub == SUB - 1, zb[1, kind, row, :], down(a, 0))

        own_ym, own_yp, oy_ym, oy_yp = up(own, 1), down(own, 1), up(oy, 1), down(oy, 1)
        oz_ym, oz_yp = up(oz, 1), down(oz, 1)
        own_zm, own_zp = z_before(own, OWN), z_after(own, OWN)
        oy_zm, oy_zp = z_before(oy, OY), z_after(oy, OY)
        oz_zm, oz_zp = z_before(oz, OZ), z_after(oz, OZ)
        tymc, typc = only(cross_ym, tym), only(cross_yp, typ)
        tzmc, tzpc = only(cross_zm, tzm), only(cross_zp, tzp)
        tymn, typn, tzmn, tzpn = tym - tymc, typ - typc, tzm - tzmc, tzp - tzpc
        before_own = ox_s[plane(0), :] if edge < 0 else own_s[at, :]
        after_own = ox_s[plane(3), :] if edge > 0 else own_s[after, :]
        q0 = (
            diagonal * own - txm * before_own - txp * after_own
            - tymc * oy_ym - tymn * own_ym - typc * oy_yp - typn * own_yp
            - tzmc * oz_zm - tzmn * own_zm - tzpc * oz_zp - tzpn * own_zp
        )
        qy = (
            diagonal * oy - tymc * own_ym - tymn * oy_ym - typc * own_yp - typn * oy_yp
            - tzmn * oy_zm - tzpn * oy_zp
        )
        qz = (
            diagonal * oz - tzmc * own_zm - tzmn * oz_zm - tzpc * own_zp - tzpn * oz_zp
            - tymn * oz_ym - typn * oz_yp
        )
        if edge >= 0:
            qy = qy - txm * oy_s[at, :]
            qz = qz - txm * oz_s[at, :]
        if edge <= 0:
            qy = qy - txp * oy_s[after, :]
            qz = qz - txp * oz_s[after, :]
        qzy = -(tymc * oz_ym + typc * oz_yp + tzmc * oy_zm + tzpc * oy_zp)
        fields = list(zip(FULL_OFFSETS, (q0, qy, qz, qzy, source)))
        weights = ((OWN, own), (OZ, oz), (OY, oy))
        for kind, weight in weights:
            for offset, field in fields:
                add((kind, offset, 0), weight * field)
        if not edge:
            return
        ox = ox_s[plane(1 if edge < 0 else 2), :]
        if edge < 0:
            for offset, field in fields:
                add((OX, offset, -1), ox * field)
            across, t_across = plane(0), txm
        else:
            add((OX, None, 1), ox * source)
            across, t_across = plane(nx + 1), txp
        ox_ym, ox_yp = up(ox, 1), down(ox, 1)
        ox_zm, ox_zp = z_before(ox, OX), z_after(ox, OX)
        qx = (
            diagonal * ox - t_across * own_s[across, :]
            - tymn * ox_ym - typn * ox_yp - tzmn * ox_zm - tzpn * ox_zp
        )
        qxy = -(t_across * oy_s[across, :] + tymc * ox_ym + typc * ox_yp)
        qxz = -(t_across * oz_s[across, :] + tzmc * ox_zm + tzpc * ox_zp)
        for offset, field in zip(EDGE_OFFSETS, (qx, qxy, qxz)):
            add((OX, offset, edge), ox * field)
            if edge > 0:
                for kind, weight in weights:
                    add((kind, offset, 1), weight * field)
        if edge > 0:
            inward = -txm * ox
            for kind, ref in ((OWN, own_s), (OZ, oz_s), (OY, oy_s)):
                add((kind, EDGE_OFFSETS[0], 1), ref[at, :] * inward)

    products(0, -1)
    lax.fori_loop(1, nx - 1, lambda i, c: (products(i, 0), c)[1], 0)
    products(nx - 1, 1)

    fine = lax.broadcasted_iota(jnp.int32, (ny, LANES), 0)
    spot = lax.broadcasted_iota(jnp.int32, (ny, LANES), 1)
    group = spot // cells
    upper = group % 2
    wanted = fine // EDGE + jnp.where(group >= 2, 2 * upper - 1, 0)
    hit = (fine // HALF % 2 == upper) & (wanted == spot % cells) & (group < 4)
    gather = jnp.where(hit, 1.0, 0.0).astype(jnp.bfloat16)
    halves = split_dot(gather, acc[...], swap=True)
    sums = halves.reshape(PADDED, SUB, LANES).sum(axis=1)
    stacked = jnp.concatenate(
        [sums] + [pltpu.roll(sums, LANES - g * cells, 1) for g in (1, 2, 3)], axis=0
    )
    routed = split_dot(route[...], stacked)
    routed = jnp.where(
        lax.broadcasted_iota(jnp.int32, routed.shape, 1) < cells, routed, 0.0
    )
    beside_pair = pair + 2 * parity - 1
    near_pair = jnp.clip(beside_pair, 0, pairs - 1)
    for target in range(6):
        block = routed[target * VALUES : (target + 1) * VALUES, :]
        if rows < VALUES:
            block = block[:rows, :] + pltpu.roll(block[rows:, :], span, 1)
        to_pair = near_pair if target % 2 else pair
        part[target] = pltpu.roll(block, to_pair * cells, 1)

    def fold_copy(sx, beside, which):
        to_pair = beside_pair if beside else pair
        role = layer - 2 * to_pair + 1
        slot = (1 - sx) * 4 + role
        n = ((sx + 1) * 2 + beside) * 2 + which
        return pltpu.make_async_remote_copy(
            part.at[(sx + 1) * 2 + beside], fold.at[slot], f_send.at[n], f_recv.at[slot],
            device_id=(tile + sx, 2 * to_pair + which), device_id_type=MESH,
        )

    def fold_valid(sx, beside, which):
        ok = (tile + sx >= 0) & (tile + sx < tiles)
        if beside:
            return ok & (beside_pair >= 0) & (beside_pair < pairs)
        return ok if sx else ok & (which != parity)

    fold_list = [(sx, b, w) for b in (1, 0) for sx in (-1, 1, 0) for w in (0, 1)]
    for item in fold_list:
        @pl.when(fold_valid(*item))
        def _():
            fold_copy(*item).start()

    gsend[...] = part[2]
    for dt in (-1, 0, 1):
        for role in range(4):
            from_layer = 2 * pair - 1 + role
            ok = (tile + dt >= 0) & (tile + dt < tiles)
            ok = ok & (from_layer >= 0) & (from_layer < layers)
            if dt == 0:
                ok = ok & (from_layer != layer)
            slot = (dt + 1) * 4 + role

            @pl.when(ok)
            def _():
                pltpu.make_async_remote_copy(
                    part.at[0], fold.at[slot], f_send.at[0], f_recv.at[slot],
                    device_id=(tile, layer), device_id_type=MESH,
                ).wait_recv()
                gsend[...] = gsend[...] + fold[slot]

    def gather_copy(k):
        other = lax.rem(tile * pairs + pair + k, tiles * pairs)
        return pltpu.make_async_remote_copy(
            gsend, gath.at[tile * pairs + pair], g_send.at[k], g_recv.at[tile * pairs + pair],
            device_id=(other // pairs, 2 * (other % pairs) + parity), device_id_type=MESH,
        )

    for k in range(1, tiles * pairs):
        gather_copy(k).start()
    gath[tile * pairs + pair] = gsend[...]

    cell_at = lax.broadcasted_iota(jnp.int32, (LANES, ny), 0)
    fine_at = lax.broadcasted_iota(jnp.int32, (LANES, ny), 1)
    parent = fine_at // EDGE
    spread = jnp.where(cell_at == parent, 1.0, 0.0).astype(jnp.bfloat16)
    beside_y = parent + 2 * (fine_at // HALF % 2) - 1
    spread_y = jnp.where(cell_at == beside_y, 1.0, 0.0).astype(jnp.bfloat16)

    for k in range(1, tiles * pairs):
        frm = lax.rem(tile * pairs + pair + tiles * pairs - k, tiles * pairs)
        pltpu.make_async_remote_copy(
            gsend, gath.at[frm], g_send.at[k], g_recv.at[frm],
            device_id=(tile, layer), device_id_type=MESH,
        ).wait_recv()

    for t in range(tiles):
        total = gath[t * pairs]
        for p in range(1, pairs):
            total = total + gath[t * pairs + p]
        gsum[pl.ds(t * rows, rows), :] = total
    lane_t = lax.broadcasted_iota(jnp.int32, (tiles, LANES), 1)

    def value(v):
        a = gsum[pl.ds(v % rows, tiles, stride=rows), :]
        if v >= rows:
            a = pltpu.roll(a, LANES - span, 1)
        return only(lane_t < span, a)

    def shifted(a, offset):
        ox, oz, oy = offset
        along = -(oz * cells + oy) % LANES
        if along:
            a = pltpu.roll(a, along, 1)
        if ox:
            a = pltpu.roll(a, -ox % tiles, 0)
        return a

    offsets = [((v + 13) // 9 - 1, (v + 13) // 3 % 3 - 1, (v + 13) % 3 - 1) for v in range(14)]
    forward = [value(v) for v in range(14)]
    backward = [
        shifted(forward[v], [-d for d in offsets[v]]) if v else None for v in range(14)
    ]
    rhs = value(RHS)
    scale = COARSE_DAMPING / jnp.where(lane_t < span, forward[0], 1.0)
    coarse = rhs * scale
    for _ in range(SWEEPS - 1):
        applied = forward[0] * coarse
        for v in range(1, 14):
            applied = applied + forward[v] * shifted(coarse, offsets[v])
            applied = applied + backward[v] * shifted(coarse, [-d for d in offsets[v]])
        coarse = coarse + (rhs - applied) * scale
    csc[...] = coarse

    def coarse_row(t, p):
        a = jnp.broadcast_to(csc[pl.ds(t, 1), :], (SUB, LANES))
        return pltpu.roll(a, (LANES - p * cells) % LANES, 1)

    center = coarse_row(tile, pair)
    four = jnp.concatenate(
        [
            center,
            coarse_row(tile, near_pair),
            coarse_row(jnp.maximum(tile - 1, 0), pair),
            coarse_row(jnp.minimum(tile + 1, tiles - 1), pair),
        ],
        axis=0,
    )
    wide = split_dot(spread, four, swap=True)
    c_own, c_z = wide[:SUB, :], wide[SUB : 2 * SUB, :]
    c_y = split_dot(spread_y, center, swap=True)
    for i in range(nx):
        at = plane(i + 1)
        result = own_s[at, :] * c_own + oz_s[at, :] * c_z + oy_s[at, :] * c_y
        if i == 0:
            result = result + ox_s[plane(1), :] * wide[2 * SUB : 3 * SUB, :]
        if i == nx - 1:
            result = result + ox_s[plane(2), :] * wide[3 * SUB :, :]
        out_ref[plane(i), :] = result

    for sz in sides:
        @pl.when(has(0, sz))
        def _():
            layer_copy(sz).wait_send()
    for sx in sides:
        @pl.when(has(sx, 0))
        def _():
            for copy in halo_copies(sx):
                copy.wait_send()
    for sx, sz in diagonals:
        @pl.when(has(sx, sz))
        def _():
            corner_copy(sx, sz).wait_send()
    for item in fold_list:
        @pl.when(fold_valid(*item))
        def _():
            fold_copy(*item).wait_send()
    for k in range(1, tiles * pairs):
        gather_copy(k).wait_send()


def body(tiles, layers, classes, well_mask, source):
    nx, nz, ny = classes.shape
    assert nx == EDGE and nz == HALF == SUB and layers % 2 == 0
    cells, pairs = ny // EDGE, layers // 2
    assert 4 * cells <= LANES and pairs * cells <= LANES
    rows = VALUES // 2 if 2 * pairs * cells <= LANES else VALUES
    flat = lambda a: a.reshape(nx * nz, ny)
    f32 = lambda *shape: pltpu.VMEM(shape, jnp.float32)
    dma = pltpu.SemaphoreType.DMA
    block = (nx * SUB, ny)
    wide = ((nx + 2) * SUB, ny)
    scratch = [
        pltpu.VMEM(block, jnp.int32), pltpu.VMEM(block, jnp.int32), f32(*block),
        pltpu.VMEM((6 * VALUES, 4 * PADDED), jnp.bfloat16),
        f32((nx + 4) * SUB, ny), f32(*wide), f32(2, 3, nx, ny), f32(2, 3, nx, ny),
        f32(4, 1, ny), f32(4, 1, ny),
        f32(*block), f32(*block), f32((nx + 1) * SUB, ny), f32(*block), f32(*block), f32(*block),
        f32(*wide), f32(*wide), f32(*wide), f32(4 * SUB, ny), f32(2, nx, ny), f32(2, 4, nx, ny),
        pltpu.VMEM((3, nx, ny), jnp.int32), f32(PADDED * SUB, ny), f32(6, rows, LANES), f32(12, rows, LANES), f32(rows, LANES),
        f32(tiles * pairs, rows, LANES), f32(tiles * rows, LANES), f32(tiles, LANES),
        dma((4,)), dma((2, 2)), dma((2, 2)), dma((2,)), dma((2,)), dma((4,)), dma((4,)),
        dma((12,)), dma((12,)), dma((tiles * pairs,)), dma((tiles * pairs,)),
    ]
    route = jnp.asarray(routing_table(), jnp.bfloat16)
    result = pl.pallas_call(
        functools.partial(kernel, tiles, layers, nx, ny),
        out_shape=jax.ShapeDtypeStruct(block, jnp.float32),
        in_specs=[pl.BlockSpec(memory_space=pl.ANY)] * 4,
        out_specs=pl.BlockSpec(memory_space=pltpu.VMEM),
        scratch_shapes=scratch,
        compiler_params=pltpu.CompilerParams(
            collective_id=0, has_side_effects=True, vmem_limit_bytes=32 * 2**20
        ),
    )(flat(classes), flat(well_mask), flat(source), route)
    return result.reshape(nx, nz, ny)


def solution(mesh):
    spec = P("tile", "layer", None)
    return jax.shard_map(
        functools.partial(body, mesh.shape["tile"], mesh.shape["layer"]),
        mesh=mesh, in_specs=(spec, spec, spec), out_specs=spec, check_vma=False,
    )
```

time: 171 us -> 29.6 us (0.17)
  the two profiles are of different devices: /device:TPU:3 before, /device:TPU:0 now
where the time goes in v1:
time: 29.6 us; the launch traced here: 29.3 us
  Pallas kernels  24.9 us (84%)
  local copies, waits for them, and re-layouts  4.45 us (15%)
    pallas_call x1, Pallas kernels, body(): pl.pallas_call(functools.partial(kernel, tiles, layers, nx, ny), out_shap...  24.9 us
    unnamed x9, local copies, waits for them, and re-layouts  4.45 us

profile of v1, /device:TPU:0, one launch (start us, length us, event | category | flops | bytes accessed | tf_op | source)
XLA Modules:
  0.0 29.3 jit_solution(10945961444916792333)
XLA Ops:
  0.0 0.0 copy-start
  0.0 0.9 %copy-done = s32[16,8,512]{2,1,0:T(8,128)S(1)} copy-done((s32[16,8,512]{2,1,0:T(8,128)S(1)}, s32[16,8,512]{2,1,0:T(8,128)}, u32[]{:S(2)}) %copy-start) | copy-done | bytes 262168
  1.0 0.0 copy-start.1
  1.0 0.9 %copy-done.1 = s32[16,8,512]{2,1,0:T(8,128)S(1)} copy-done((s32[16,8,512]{2,1,0:T(8,128)S(1)}, s32[16,8,512]{2,1,0:T(8,128)}, u32[]{:S(2)}) %copy-start.1) | copy-done | bytes 262168
  1.9 0.0 copy-start.2
  1.9 0.9 %copy-done.2 = f32[16,8,512]{2,1,0:T(8,128)S(1)} copy-done((f32[16,8,512]{2,1,0:T(8,128)S(1)}, f32[16,8,512]{2,1,0:T(8,128)}, u32[]{:S(2)}) %copy-start.2) | copy-done | bytes 262168
  2.9 0.0 copy-start.3
  2.9 0.9 %copy-done.3 = bf16[2,96,160]{2,1,0:T(8,128)(2,1)S(1)} copy-done((bf16[2,96,160]{2,1,0:T(8,128)(2,1)S(1)}, bf16[2,96,160]{2,1,0:T(8,128)(2,1)}, u32[]{:S(2)}) %copy-start.3) | copy-done | bytes 61464
  3.7 24.9 %shard_map.46 = f32[128,512]{1,0:T(8,128)S(1)} custom-call(s32[128,512]{1,0:T(8,128)S(1)} %bitcast.5, s32[128,512]{1,0:T(8,128)S(1)} %bitcast.6, f32[128,512]{1,0:T(8,128)S(1)} %bitcast.7, bf16[2,96,160]{2,1,0:T(8,128)(2,1)S(1)} %copy-done.3), custom_call_target="tpu_custom_call" | custom-call | tf_op jit(solution)/shard_map/pallas_call | solution.py:668
  28.6 0.7 %copy.6 = f32[16,8,512]{2,1,0:T(8,128)} copy(f32[16,8,512]{2,1,0:T(8,128)S(1)} %bitcast.4) | data formatting | bytes 524288
Async XLA Ops:
  0.0 0.9 %copy-start = (s32[16,8,512]{2,1,0:T(8,128)S(1)}, s32[16,8,512]{2,1,0:T(8,128)}, u32[]{:S(2)}) copy-start(s32[16,8,512]{2,1,0:T(8,128)} %param.4) | copy-start | bytes 786436
  1.0 0.9 %copy-start.1 = (s32[16,8,512]{2,1,0:T(8,128)S(1)}, s32[16,8,512]{2,1,0:T(8,128)}, u32[]{:S(2)}) copy-start(s32[16,8,512]{2,1,0:T(8,128)} %param.5) | copy-start | bytes 786436
  1.9 0.9 %copy-start.2 = (f32[16,8,512]{2,1,0:T(8,128)S(1)}, f32[16,8,512]{2,1,0:T(8,128)}, u32[]{:S(2)}) copy-start(f32[16,8,512]{2,1,0:T(8,128)} %param.6) | copy-start | bytes 786436
  2.9 0.9 %copy-start.3 = (bf16[2,96,160]{2,1,0:T(8,128)(2,1)S(1)}, bf16[2,96,160]{2,1,0:T(8,128)(2,1)}, u32[]{:S(2)}) copy-start(bf16[2,96,160]{2,1,0:T(8,128)(2,1)} %constant.2.clone.route_hbm) | copy-start | bytes 184324

commit v2 on v1

--- a/solution.py
+++ b/solution.py
@@ -232,31 +232,24 @@
     def only(mask, a):
         return jnp.where(mask, a, 0.0)
 
-    def early(i, carry):
-        at = pl.ds(pl.multiple_of(i * SUB, SUB), SUB)
-        k = perm_of(cls[at, :])
-        kx[pl.ds(pl.multiple_of((i + 2) * SUB, SUB), SUB), :] = k
-        sk[pl.ds(pl.multiple_of((i + 1) * SUB, SUB), SUB), :] = sink_of(well[at, :], k)
-        return carry
-
-    lax.fori_loop(2, nx - 2, early, 0)
+    for i in range(2, nx - 2):
+        k = perm_of(cls[plane(i), :])
+        kx[plane(i + 2), :] = k
+        sk[plane(i + 1), :] = sink_of(well[plane(i), :], k)
     for i in (1, nx - 2):
         sk[plane(i + 1), :] = sink_of(well[plane(i), :], kx[plane(i + 2), :])
 
-    def faces(i, carry):
-        at = pl.ds(pl.multiple_of(i * SUB, SUB), SUB)
-        k = kx[pl.ds(pl.multiple_of((i + 2) * SUB, SUB), SUB), :]
+    def faces(i):
+        at = plane(i)
+        k = kx[plane(i + 2), :]
         typ_s[at, :] = y_face(k)
         tzi_s[at, :] = VERTICAL_RATIO * harmonic(k, up(k, 0))
 
-        @pl.when(i > 0)
-        def _():
-            before = kx[pl.ds(pl.multiple_of((i + 1) * SUB, SUB), SUB), :]
-            txf[at, :] = harmonic(before, k)
-
-        return carry
-
-    lax.fori_loop(0, nx, faces, 0)
+        if i > 0:
+            txf[at, :] = harmonic(kx[plane(i + 1), :], k)
+
+    for i in range(nx):
+        faces(i)
 
     for sz in sides:
         @pl.when(has(0, sz))
@@ -343,8 +336,8 @@
         zb[side, OY] = outer[2]
 
     def block_basis(i, edge):
-        at = pl.ds(pl.multiple_of(i * SUB, SUB), SUB)
-        after = pl.ds(pl.multiple_of((i + 1) * SUB, SUB), SUB)
+        at = plane(i)
+        after = plane(i + 1)
         inner = tzi_s[at, :]
         tzm = jnp.where(sub == 0, tz_edge[0, pl.ds(i, 1), :], inner)
         tzp = jnp.where(sub == SUB - 1, tz_edge[1, pl.ds(i, 1), :], down(inner, 0))
@@ -369,9 +362,8 @@
         if edge:
             ox_s[plane(1 if edge < 0 else 2), :] = outer[0]
 
-    block_basis(0, -1)
-    lax.fori_loop(1, nx - 1, lambda i, c: (block_basis(i, 0), c)[1], 0)
-    block_basis(nx - 1, 1)
+    for i in range(nx):
+        block_basis(i, -1 if i == 0 else int(i == nx - 1))
 
     loads[2].wait()
     loads[3].wait()
@@ -383,9 +375,9 @@
         acc[at, :] = acc[at, :] + term
 
     def products(i, edge):
-        at = pl.ds(pl.multiple_of(i * SUB, SUB), SUB)
-        mid = pl.ds(pl.multiple_of((i + 1) * SUB, SUB), SUB)
-        after = pl.ds(pl.multiple_of((i + 2) * SUB, SUB), SUB)
+        at = plane(i)
+        mid = plane(i + 1)
+        after = plane(i + 2)
         row = pl.ds(i, 1)
         diagonal, tzm, tzp, typ = d_s[at, :], tzm_s[at, :], tzp_s[at, :], typ_s[at, :]
         tym = up(typ, 1)
@@ -462,9 +454,8 @@
             for kind, ref in ((OWN, own_s), (OZ, oz_s), (OY, oy_s)):
                 add((kind, EDGE_OFFSETS[0], 1), ref[at, :] * inward)
 
-    products(0, -1)
-    lax.fori_loop(1, nx - 1, lambda i, c: (products(i, 0), c)[1], 0)
-    products(nx - 1, 1)
+    for i in range(nx):
+        products(i, -1 if i == 0 else int(i == nx - 1))
 
     fine = lax.broadcasted_iota(jnp.int32, (ny, LANES), 0)
     spot = lax.broadcasted_iota(jnp.int32, (ny, LANES), 1)
@@ -668,11 +659,11 @@
     result = pl.pallas_call(
         functools.partial(kernel, tiles, layers, nx, ny),
         out_shape=jax.ShapeDtypeStruct(block, jnp.float32),
-        in_specs=[pl.BlockSpec(memory_space=pl.ANY)] * 4,
+        in_specs=[pl.BlockSpec(memory_space=pltpu.HBM)] * 4,
         out_specs=pl.BlockSpec(memory_space=pltpu.VMEM),
         scratch_shapes=scratch,
         compiler_params=pltpu.CompilerParams(
-            collective_id=0, has_side_effects=True, vmem_limit_bytes=32 * 2**20
+            collective_id=0, has_side_effects=True, vmem_limit_bytes=60 * 2**20
         ),
     )(flat(classes), flat(well_mask), flat(source), route)
     return result.reshape(nx, nz, ny)

time: 29.6 us -> 25.5 us (0.86)
  local copies, waits for them, and re-layouts: 4.45 us -> 1.67 us
  Pallas kernels: 24.9 us -> 23.7 us
    unnamed x9 -> x1, local copies, waits for them, and re-layouts: 4.45 us -> 1.67 us
    pallas_call x1, Pallas kernels: 24.9 us -> 23.7 us  [body(): pl.pallas_call(functools.partial(kernel, tiles, layers, nx, ny), out_shap...]
where the time goes in v2:
time: 25.5 us; the launch traced here: 25.4 us
  Pallas kernels  23.7 us (93%)
  local copies, waits for them, and re-layouts  1.67 us (7%)
    pallas_call x1, Pallas kernels, body(): pl.pallas_call(functools.partial(kernel, tiles, layers, nx, ny), out_shap...  23.7 us
    unnamed x1, local copies, waits for them, and re-layouts  1.67 us

profile of v2, /device:TPU:0, one launch (start us, length us, event | category | flops | bytes accessed | tf_op | source)
XLA Modules:
  0.0 25.4 jit_solution(1055968500014645610)
XLA Ops:
  0.0 23.7 %shard_map.46 = f32[128,512]{1,0:T(8,128)} custom-call(s32[128,512]{1,0:T(8,128)} %bitcast.5, s32[128,512]{1,0:T(8,128)} %bitcast.6, f32[128,512]{1,0:T(8,128)} %bitcast.7, bf16[2,96,160]{2,1,0:T(8,128)(2,1)} %constant.2.clone.route_hbm), custom_call_target="tpu_custom_call" | custom-call | tf_op jit(solution)/shard_map/pallas_call | solution.py:659
  23.7 1.7 %copy.6 = f32[16,8,512]{2,1,0:T(8,128)} copy(f32[16,8,512]{2,1,0:T(8,128)} %bitcast.4) | data formatting | bytes 524288

commit v3 on v2

--- a/solution.py
+++ b/solution.py
@@ -59,7 +59,7 @@
 def split_dot(table, values, swap=False):
     total = None
     rest = values
-    for _ in range(3):
+    for _ in range(2):
         part = rest.astype(jnp.bfloat16)
         rest = rest - part.astype(jnp.float32)
         pair = (part, table) if swap else (table, part)
@@ -85,7 +85,7 @@
     tiles, layers, nx, ny,
     cls_hbm, well_hbm, src_hbm, route_hbm, out_ref,
     cls, well, src, route,
-    kx, sk, zs, zr, crs, crr,
+    kx, sk, zs, zr, crs, crr, zq, ze,
     typ_s, tzi_s, txf, tzm_s, tzp_s, d_s, own_s, oy_s, oz_s, ox_s, tz_edge, zb,
     zi, acc, part, fold, gsend, gath, gsum, csc,
     in_sem, x_send, x_recv, z_send, z_recv, c_send, c_recv, f_send, f_recv, g_send, g_recv,
@@ -110,16 +110,25 @@
         load.start()
 
     barrier = pltpu.get_barrier_semaphore()
-    me = tile * layers + layer
-
-    def greet(k, carry):
-        other = lax.rem(me + k, tiles * layers)
-        pl.semaphore_signal(
-            barrier, inc=1, device_id=(other // layers, other % layers), device_id_type=MESH
-        )
-        return carry
-
-    lax.fori_loop(1, tiles * layers, greet, 0)
+    for a in range(tiles):
+        for b in range(layers):
+            if a or b:
+                pl.semaphore_signal(
+                    barrier, inc=1, device_id_type=MESH,
+                    device_id=(lax.rem(tile + a, tiles), lax.rem(layer + b, layers)),
+                )
+
+    def fold_from(dt, role):
+        from_layer = 2 * pair - 1 + role
+        ok = (tile + dt >= 0) & (tile + dt < tiles)
+        ok = ok & (from_layer >= 0) & (from_layer < layers)
+        return ok & (from_layer != layer) if dt == 0 else ok
+
+    for dt in (-1, 0, 1):
+        for role in range(4):
+            @pl.when(jnp.logical_not(fold_from(dt, role)))
+            def _():
+                fold[(dt + 1) * 4 + role] = jnp.zeros(fold.shape[1:], jnp.float32)
 
     loads[0].wait()
     loads[1].wait()
@@ -334,6 +343,8 @@
         zb[side, OX] = outer[0]
         zb[side, OZ] = outer[1]
         zb[side, OY] = outer[2]
+        zq[side, 0] = jnp.where(crosses, outer[1], own)
+        zq[side, 1] = jnp.where(crosses, 0.0, outer[2])
 
     def block_basis(i, edge):
         at = plane(i)
@@ -357,7 +368,8 @@
         tzp_s[at, :] = tzp
         d_s[at, :] = diagonal
         own_s[after, :] = own
-        oz_s[after, :] = outer[1]
+        if i >= nx - 2:
+            oz_s[after, :] = outer[1]
         oy_s[after, :] = outer[2]
         if edge:
             ox_s[plane(1 if edge < 0 else 2), :] = outer[0]
@@ -368,62 +380,45 @@
     loads[2].wait()
     loads[3].wait()
 
-    acc[...] = jnp.zeros(acc.shape, jnp.float32)
+    sums_of = {}
 
     def add(product, term):
-        at = plane(SLOT[product])
-        acc[at, :] = acc[at, :] + term
+        sums_of[product] = sums_of[product] + term if product in sums_of else term
 
     def products(i, edge):
-        at = plane(i)
-        mid = plane(i + 1)
-        after = plane(i + 2)
-        row = pl.ds(i, 1)
+        at, mid, after, row = plane(i), plane(i + 1), plane(i + 2), pl.ds(i, 1)
         diagonal, tzm, tzp, typ = d_s[at, :], tzm_s[at, :], tzp_s[at, :], typ_s[at, :]
         tym = up(typ, 1)
         txm, txp = txf[at, :], txf[mid, :]
-        own, oz, oy = own_s[mid, :], oz_s[mid, :], oy_s[mid, :]
+        own, oy = own_s[mid, :], oy_s[mid, :]
         source = src[at, :]
-
-        def z_before(a, kind):
-            return jnp.where(sub == 0, zb[0, kind, row, :], up(a, 0))
-
-        def z_after(a, kind):
-            return jnp.where(sub == SUB - 1, zb[1, kind, row, :], down(a, 0))
-
-        own_ym, own_yp, oy_ym, oy_yp = up(own, 1), down(own, 1), up(oy, 1), down(oy, 1)
-        oz_ym, oz_yp = up(oz, 1), down(oz, 1)
-        own_zm, own_zp = z_before(own, OWN), z_after(own, OWN)
-        oy_zm, oy_zp = z_before(oy, OY), z_after(oy, OY)
-        oz_zm, oz_zp = z_before(oz, OZ), z_after(oz, OZ)
-        tymc, typc = only(cross_ym, tym), only(cross_yp, typ)
-        tzmc, tzpc = only(cross_zm, tzm), only(cross_zp, tzp)
-        tymn, typn, tzmn, tzpn = tym - tymc, typ - typc, tzm - tzmc, tzp - tzpc
+        swap_m, swap_p = jnp.where(cross_yp, oy, own), jnp.where(cross_ym, oy, own)
+        keep_m, keep_p = jnp.where(cross_yp, own, oy), jnp.where(cross_ym, own, oy)
+
+        def z_pair(a, kind):
+            return (
+                jnp.where(sub == 0, zq[0, kind, row, :], up(a, 0)),
+                jnp.where(sub == SUB - 1, zq[1, kind, row, :], down(a, 0)),
+            )
+
+        own_zm, own_zp = z_pair(own, 0)
+        oy_zm, oy_zp = z_pair(oy, 1)
         before_own = ox_s[plane(0), :] if edge < 0 else own_s[at, :]
         after_own = ox_s[plane(3), :] if edge > 0 else own_s[after, :]
         q0 = (
             diagonal * own - txm * before_own - txp * after_own
-            - tymc * oy_ym - tymn * own_ym - typc * oy_yp - typn * own_yp
-            - tzmc * oz_zm - tzmn * own_zm - tzpc * oz_zp - tzpn * own_zp
+            - tym * up(swap_m, 1) - typ * down(swap_p, 1) - tzm * own_zm - tzp * own_zp
         )
         qy = (
-            diagonal * oy - tymc * own_ym - tymn * oy_ym - typc * own_yp - typn * oy_yp
-            - tzmn * oy_zm - tzpn * oy_zp
-        )
-        qz = (
-            diagonal * oz - tzmc * own_zm - tzmn * oz_zm - tzpc * own_zp - tzpn * oz_zp
-            - tymn * oz_ym - typn * oz_yp
+            diagonal * oy - tym * up(keep_m, 1) - typ * down(keep_p, 1)
+            - tzm * oy_zm - tzp * oy_zp
         )
         if edge >= 0:
             qy = qy - txm * oy_s[at, :]
-            qz = qz - txm * oz_s[at, :]
         if edge <= 0:
             qy = qy - txp * oy_s[after, :]
-            qz = qz - txp * oz_s[after, :]
-        qzy = -(tymc * oz_ym + typc * oz_yp + tzmc * oy_zm + tzpc * oy_zp)
-        fields = list(zip(FULL_OFFSETS, (q0, qy, qz, qzy, source)))
-        weights = ((OWN, own), (OZ, oz), (OY, oy))
-        for kind, weight in weights:
+        fields = (((0, 0, 0), q0), ((0, 0, 1), qy), (None, source))
+        for kind, weight in ((OWN, own), (OY, oy)):
             for offset, field in fields:
                 add((kind, offset, 0), weight * field)
         if not edge:
@@ -436,18 +431,21 @@
         else:
             add((OX, None, 1), ox * source)
             across, t_across = plane(nx + 1), txp
+        tymc, typc = only(cross_ym, tym), only(cross_yp, typ)
+        tzmc, tzpc = only(cross_zm, tzm), only(cross_zp, tzp)
         ox_ym, ox_yp = up(ox, 1), down(ox, 1)
-        ox_zm, ox_zp = z_before(ox, OX), z_after(ox, OX)
+        ox_zm = jnp.where(sub == 0, zb[0, OX, row, :], up(ox, 0))
+        ox_zp = jnp.where(sub == SUB - 1, zb[1, OX, row, :], down(ox, 0))
         qx = (
-            diagonal * ox - t_across * own_s[across, :]
-            - tymn * ox_ym - typn * ox_yp - tzmn * ox_zm - tzpn * ox_zp
+            diagonal * ox - t_across * own_s[across, :] - (tym - tymc) * ox_ym
+            - (typ - typc) * ox_yp - (tzm - tzmc) * ox_zm - (tzp - tzpc) * ox_zp
         )
         qxy = -(t_across * oy_s[across, :] + tymc * ox_ym + typc * ox_yp)
         qxz = -(t_across * oz_s[across, :] + tzmc * ox_zm + tzpc * ox_zp)
         for offset, field in zip(EDGE_OFFSETS, (qx, qxy, qxz)):
             add((OX, offset, edge), ox * field)
             if edge > 0:
-                for kind, weight in weights:
+                for kind, weight in ((OWN, own), (OZ, oz_s[mid, :]), (OY, oy)):
                     add((kind, offset, 1), weight * field)
         if edge > 0:
             inward = -txm * ox
@@ -456,6 +454,67 @@
 
     for i in range(nx):
         products(i, -1 if i == 0 else int(i == nx - 1))
+
+    z1 = parity * (SUB - 1)
+    z2 = 1 + parity * (SUB - 3)
+    for i in range(nx):
+        ze[1, pl.ds(i, 1), :] = own_s[pl.ds((i + 1) * SUB + z2, 1), :]
+        ze[2, pl.ds(i, 1), :] = oy_s[pl.ds((i + 1) * SUB + z2, 1), :]
+        ze[3, pl.ds(i, 1), :] = src[pl.ds(i * SUB + z1, 1), :]
+    first, last = wide_row == 0, wide_row == nx - 1
+    wide_ym, wide_yp = wide_lane % EDGE == 0, wide_lane % EDGE == EDGE - 1
+    k1 = zs[parity, 0]
+    t_out = tz_edge[parity]
+    t_in = VERTICAL_RATIO * harmonic(k1, zs[parity, 1])
+    inner = harmonic(k1, up(k1, 0))
+    txm = jnp.where(first, harmonic(k1, kx[pl.ds(SUB + z1, 1), :]), inner)
+    txp = jnp.where(last, harmonic(k1, kx[pl.ds((nx + 2) * SUB + z1, 1), :]), down(inner, 0))
+    typ = y_face(k1)
+    tym = up(typ, 1)
+    txmc, txpc = only(first, txm), only(last, txp)
+    tymc, typc = only(wide_ym, tym), only(wide_yp, typ)
+    diagonal, own, (ox, oz, oy) = basis(
+        zs[parity, 2], ((txm, txp), (t_in, t_out), (tym, typ)),
+        (txmc + txpc, t_out, tymc + typc),
+    )
+    ze[0] = oz
+    txmn, txpn, tymn, typn = txm - txmc, txp - txpc, tym - tymc, typ - typc
+    own_in, oy_in, source = ze[1], ze[2], ze[3]
+    ox_before, ox_after = ox_s[pl.ds(z1, 1), :], ox_s[pl.ds(3 * SUB + z1, 1), :]
+    oz_ym, oz_yp = up(oz, 1), down(oz, 1)
+    q0 = (
+        diagonal * own - t_out * zb[parity, OZ] - t_in * own_in
+        - txm * jnp.where(first, ox_before, up(own, 0))
+        - txp * jnp.where(last, ox_after, down(own, 0))
+        - tym * up(jnp.where(wide_yp, oy, own), 1) - typ * down(jnp.where(wide_ym, oy, own), 1)
+    )
+    qy = (
+        diagonal * oy - t_in * oy_in - txmn * up(oy, 0) - txpn * down(oy, 0)
+        - tym * up(jnp.where(wide_yp, own, oy), 1) - typ * down(jnp.where(wide_ym, own, oy), 1)
+    )
+    qz = (
+        diagonal * oz - t_out * zb[parity, OWN] - txmn * up(oz, 0) - txpn * down(oz, 0)
+        - tymn * oz_ym - typn * oz_yp
+    )
+    qz_in = -t_in * oz
+    qzy = -(tymc * oz_ym + typc * oz_yp + t_out * zb[parity, OY])
+
+    def add_rows(product, term):
+        add(product, term[:SUB, :] + term[SUB:, :])
+
+    for offset, field in zip(FULL_OFFSETS, (q0, qy, qz, qzy, source)):
+        add_rows((OZ, offset, 0), oz * field)
+    add_rows((OWN, FULL_OFFSETS[2], 0), own * qz + own_in * qz_in)
+    add_rows((OY, FULL_OFFSETS[2], 0), oy * qz + oy_in * qz_in)
+    add_rows((OWN, FULL_OFFSETS[3], 0), own * qzy)
+    add_rows((OY, FULL_OFFSETS[3], 0), oy * qzy)
+    add_rows((OX, FULL_OFFSETS[3], -1), only(first, ox * qzy))
+    ox_in = only(first, ox_s[pl.ds(SUB + z2, 1), :])
+    add_rows((OX, FULL_OFFSETS[2], -1), only(first, ox * qz) + ox_in * qz_in)
+    for n in range(PADDED):
+        acc[plane(n), :] = (
+            sums_of[PRODUCTS[n]] if n < len(PRODUCTS) else jnp.zeros((SUB, ny), jnp.float32)
+        )
 
     fine = lax.broadcasted_iota(jnp.int32, (ny, LANES), 0)
     spot = lax.broadcasted_iota(jnp.int32, (ny, LANES), 1)
@@ -504,23 +563,21 @@
         def _():
             fold_copy(*item).start()
 
-    gsend[...] = part[2]
     for dt in (-1, 0, 1):
         for role in range(4):
-            from_layer = 2 * pair - 1 + role
-            ok = (tile + dt >= 0) & (tile + dt < tiles)
-            ok = ok & (from_layer >= 0) & (from_layer < layers)
-            if dt == 0:
-                ok = ok & (from_layer != layer)
             slot = (dt + 1) * 4 + role
 
-            @pl.when(ok)
+            @pl.when(fold_from(dt, role))
             def _():
                 pltpu.make_async_remote_copy(
                     part.at[0], fold.at[slot], f_send.at[0], f_recv.at[slot],
                     device_id=(tile, layer), device_id_type=MESH,
                 ).wait_recv()
-                gsend[...] = gsend[...] + fold[slot]
+
+    terms = [part[2]] + [fold[slot] for slot in range(12)]
+    while len(terms) > 1:
+        terms = [sum(terms[n + 1 : n + 2], terms[n]) for n in range(0, len(terms), 2)]
+    gsend[...] = terms[0]
 
     def gather_copy(k):
         other = lax.rem(tile * pairs + pair + k, tiles * pairs)
@@ -602,9 +659,12 @@
     wide = split_dot(spread, four, swap=True)
     c_own, c_z = wide[:SUB, :], wide[SUB : 2 * SUB, :]
     c_y = split_dot(spread_y, center, swap=True)
+    ze[0] = ze[0] * jnp.concatenate([c_z] * (nx // SUB), axis=0)
+    at_edge = sub == parity * (SUB - 1)
     for i in range(nx):
         at = plane(i + 1)
-        result = own_s[at, :] * c_own + oz_s[at, :] * c_z + oy_s[at, :] * c_y
+        result = own_s[at, :] * c_own + oy_s[at, :] * c_y
+        result = result + only(at_edge, ze[0, pl.ds(i, 1), :])
         if i == 0:
             result = result + ox_s[plane(1), :] * wide[2 * SUB : 3 * SUB, :]
         if i == nx - 1:
@@ -648,6 +708,7 @@
         pltpu.VMEM((6 * VALUES, 4 * PADDED), jnp.bfloat16),
         f32((nx + 4) * SUB, ny), f32(*wide), f32(2, 3, nx, ny), f32(2, 3, nx, ny),
         f32(4, 1, ny), f32(4, 1, ny),
+        f32(2, 2, nx, ny), f32(4, nx, ny),
         f32(*block), f32(*block), f32((nx + 1) * SUB, ny), f32(*block), f32(*block), f32(*block),
         f32(*wide), f32(*wide), f32(*wide), f32(4 * SUB, ny), f32(2, nx, ny), f32(2, 4, nx, ny),
         pltpu.VMEM((3, nx, ny), jnp.int32), f32(PADDED * SUB, ny), f32(6, rows, LANES), f32(12, rows, LANES), f32(rows, LANES),
@@ -663,7 +724,7 @@
         out_specs=pl.BlockSpec(memory_space=pltpu.VMEM),
         scratch_shapes=scratch,
         compiler_params=pltpu.CompilerParams(
-            collective_id=0, has_side_effects=True, vmem_limit_bytes=60 * 2**20
+            collective_id=0, has_side_effects=True, vmem_limit_bytes=107 * 2**19
         ),
     )(flat(classes), flat(well_mask), flat(source), route)
     return result.reshape(nx, nz, ny)

time: 25.5 us -> 23.8 us (0.933)
  Pallas kernels: 23.7 us -> 22 us
    pallas_call x1, Pallas kernels: 23.7 us -> 22 us  [body(): pl.pallas_call(functools.partial(kernel, tiles, layers, nx, ny), out_shap...]
    unnamed x1 -> x3, local copies, waits for them, and re-layouts: 1.67 us -> 1.6 us
where the time goes in v3:
time: 23.8 us; the launch traced here: 23.6 us
  Pallas kernels  22 us (92%)
  local copies, waits for them, and re-layouts  1.6 us (7%)
    pallas_call x1, Pallas kernels, body(): pl.pallas_call(functools.partial(kernel, tiles, layers, nx, ny), out_shap...  22 us
    unnamed x3, local copies, waits for them, and re-layouts  1.6 us

profile of v3, /device:TPU:0, one launch (start us, length us, event | category | flops | bytes accessed | tf_op | source)
XLA Modules:
  0.0 23.6 jit_solution(4572061800340776192)
XLA Ops:
  0.0 0.0 copy-start
  0.0 0.9 %copy-done = bf16[2,96,160]{2,1,0:T(8,128)(2,1)S(1)} copy-done((bf16[2,96,160]{2,1,0:T(8,128)(2,1)S(1)}, bf16[2,96,160]{2,1,0:T(8,128)(2,1)}, u32[]{:S(2)}) %copy-start) | copy-done | bytes 61464
  0.9 22.0 %shard_map.46 = f32[128,512]{1,0:T(8,128)S(1)} custom-call(s32[128,512]{1,0:T(8,128)} %bitcast.5, s32[128,512]{1,0:T(8,128)} %bitcast.6, f32[128,512]{1,0:T(8,128)} %bitcast.7, bf16[2,96,160]{2,1,0:T(8,128)(2,1)S(1)} %copy-done), custom_call_target="tpu_custom_call" | custom-call | tf_op jit(solution)/shard_map/pallas_call | solution.py:720
  22.9 0.7 %copy.6 = f32[16,8,512]{2,1,0:T(8,128)} copy(f32[16,8,512]{2,1,0:T(8,128)S(1)} %bitcast.4) | data formatting | bytes 524288
Async XLA Ops:
  0.0 0.9 %copy-start = (bf16[2,96,160]{2,1,0:T(8,128)(2,1)S(1)}, bf16[2,96,160]{2,1,0:T(8,128)(2,1)}, u32[]{:S(2)}) copy-start(bf16[2,96,160]{2,1,0:T(8,128)(2,1)} %constant.2.clone.route_hbm) | copy-start | bytes 184324

commit v4 on v3

--- a/solution.py
+++ b/solution.py
@@ -68,8 +68,14 @@
     return total
 
 
+def inverse_of(a):
+    guarded = jnp.maximum(a, 1e-30)
+    guess = pl.reciprocal(guarded, approx=True)
+    return guess * (2.0 - guarded * guess)
+
+
 def harmonic(a, b):
-    return 2.0 * a * b / jnp.maximum(a + b, 1e-30)
+    return 2.0 * a * b * inverse_of(a + b)
 
 
 def perm_of(classes):
@@ -87,7 +93,7 @@
     cls, well, src, route,
     kx, sk, zs, zr, crs, crr, zq, ze,
     typ_s, tzi_s, txf, tzm_s, tzp_s, d_s, own_s, oy_s, oz_s, ox_s, tz_edge, zb,
-    zi, acc, part, fold, gsend, gath, gsum, csc,
+    zi, half_table, acc, part, fold, gsend, gath, gsum, csc,
     in_sem, x_send, x_recv, z_send, z_recv, c_send, c_recv, f_send, f_recv, g_send, g_recv,
 ):
     tile = lax.axis_index("tile")
@@ -106,8 +112,8 @@
             ((cls_hbm, cls), (well_hbm, well), (src_hbm, src), (route_hbm.at[parity], route))
         )
     ]
-    for load in loads:
-        load.start()
+    loads[0].start()
+    loads[1].start()
 
     barrier = pltpu.get_barrier_semaphore()
     for a in range(tiles):
@@ -132,6 +138,8 @@
 
     loads[0].wait()
     loads[1].wait()
+    loads[2].start()
+    loads[3].start()
 
     for i in (0, 1, nx - 2, nx - 1):
         k = perm_of(cls[plane(i), :])
@@ -167,10 +175,10 @@
             for n, (a, b) in enumerate(((src_k, dst_k), (src_s, dst_s)))
         ]
 
-    def layer_copy(sz):
+    def layer_copy(sz, n):
         s = 0 if sz < 0 else 1
         return pltpu.make_async_remote_copy(
-            zs.at[s], zr.at[1 - s], z_send.at[s], z_recv.at[s],
+            zs.at[s, n], zr.at[1 - s, n], z_send.at[s, n], z_recv.at[s, n],
             device_id=(tile, layer + sz), device_id_type=MESH,
         )
 
@@ -195,7 +203,7 @@
     for sz in sides:
         @pl.when(has(0, sz))
         def _():
-            layer_copy(sz).start()
+            layer_copy(sz, 0).start()
 
         @pl.when(jnp.logical_not(has(0, sz)))
         def _():
@@ -219,6 +227,11 @@
         @pl.when(jnp.logical_not(has(sx, sz)))
         def _():
             crr[2 * (0 if sx < 0 else 1) + (0 if sz < 0 else 1)] = jnp.zeros((1, ny), jnp.float32)
+    for sz in sides:
+        @pl.when(has(0, sz))
+        def _():
+            layer_copy(sz, 1).start()
+            layer_copy(sz, 2).start()
 
     sub = lax.broadcasted_iota(jnp.int32, (SUB, ny), 0)
     lane = lax.broadcasted_iota(jnp.int32, (SUB, ny), 1)
@@ -260,91 +273,41 @@
     for i in range(nx):
         faces(i)
 
-    for sz in sides:
-        @pl.when(has(0, sz))
-        def _():
-            layer_copy(-sz).wait_recv()
+    fine = lax.broadcasted_iota(jnp.int32, (ny, LANES), 0)
+    spot = lax.broadcasted_iota(jnp.int32, (ny, LANES), 1)
+    group = spot // cells
+    upper = group % 2
+    wanted = fine // EDGE + jnp.where(group >= 2, 2 * upper - 1, 0)
+    hit = (fine // HALF % 2 == upper) & (wanted == spot % cells) & (group < 4)
+    half_table[...] = jnp.where(hit, 1.0, 0.0).astype(jnp.bfloat16)
+
+    def wait_layers(n):
+        for sz in sides:
+            @pl.when(has(0, sz))
+            def _():
+                layer_copy(-sz, n).wait_recv()
+
+    wait_layers(0)
     for sx in sides:
         @pl.when(has(sx, 0))
         def _():
-            for copy in halo_copies(-sx):
-                copy.wait_recv()
-    for sx, sz in diagonals:
-        @pl.when(has(sx, sz))
-        def _():
-            corner_copy(-sx, -sz).wait_recv()
+            halo_copies(-sx)[0].wait_recv()
+    txf[plane(0), :] = harmonic(kx[plane(1), :], kx[plane(2), :])
+    txf[plane(nx), :] = harmonic(kx[plane(nx + 1), :], kx[plane(nx + 2), :])
+    for side in (0, 1):
+        tz_edge[side] = VERTICAL_RATIO * harmonic(zs[side, 0], zr[side, 0])
 
     def basis(sink, faces, crossing):
         diagonal = sink
         for pair_of in faces:
             diagonal = diagonal + pair_of[0] + pair_of[1]
-        inverse = FINE_DAMPING / jnp.maximum(diagonal, 1e-30)
+        inverse = FINE_DAMPING * inverse_of(diagonal)
         leaving = sink
         for term in crossing:
             if term is not None:
                 leaving = leaving + term
         outer = [None if term is None else term * inverse for term in crossing]
         return diagonal, 1.0 - leaving * inverse, outer
-
-    for side in (0, 1):
-        k0 = kx[plane(2 if side == 0 else nx + 1), :]
-        k1 = kx[plane(1 if side == 0 else nx + 2), :]
-        k2 = kx[plane(0 if side == 0 else nx + 3), :]
-        toward = harmonic(k0, k1)
-        txf[plane(0 if side == 0 else nx), :] = toward
-        inner = VERTICAL_RATIO * harmonic(k1, up(k1, 0))
-        tzm = jnp.where(sub == 0, VERTICAL_RATIO * harmonic(k1, crr[2 * side]), inner)
-        tzp = jnp.where(
-            sub == SUB - 1, VERTICAL_RATIO * harmonic(k1, crr[2 * side + 1]), down(inner, 0)
-        )
-        typ = y_face(k1)
-        tym = up(typ, 1)
-        crossing = (
-            toward,
-            only(cross_zm, tzm) + only(cross_zp, tzp),
-            only(cross_ym, tym) + only(cross_yp, typ),
-        )
-        _, own, outer = basis(
-            sk[plane(0 if side == 0 else nx + 1), :],
-            ((toward, harmonic(k1, k2)), (tzm, tzp), (tym, typ)),
-            crossing,
-        )
-        at = plane(0 if side == 0 else nx + 1)
-        own_s[at, :] = own
-        ox_s[plane(0 if side == 0 else 3), :] = outer[0]
-        oz_s[at, :] = outer[1]
-        oy_s[at, :] = outer[2]
-
-    wide_row = lax.broadcasted_iota(jnp.int32, (nx, ny), 0)
-    wide_lane = lax.broadcasted_iota(jnp.int32, (nx, ny), 1)
-    for side in (0, 1):
-        k0 = zs[side, 0]
-        k1 = zr[side, 0]
-        k2 = zr[side, 1]
-        toward = VERTICAL_RATIO * harmonic(k0, k1)
-        tz_edge[side] = toward
-        inner = harmonic(k1, up(k1, 0))
-        txm = jnp.where(wide_row == 0, harmonic(k1, crr[side]), inner)
-        txp = jnp.where(wide_row == nx - 1, harmonic(k1, crr[2 + side]), down(inner, 0))
-        typ = y_face(k1)
-        tym = up(typ, 1)
-        crosses = even if side == 0 else jnp.logical_not(even)
-        crossing = (
-            only(wide_row == 0, txm) + only(wide_row == nx - 1, txp),
-            toward * crosses.astype(jnp.float32),
-            only(wide_lane % EDGE == 0, tym) + only(wide_lane % EDGE == EDGE - 1, typ),
-        )
-        _, own, outer = basis(
-            zr[side, 2],
-            ((txm, txp), (toward, VERTICAL_RATIO * harmonic(k1, k2)), (tym, typ)),
-            crossing,
-        )
-        zb[side, OWN] = own
-        zb[side, OX] = outer[0]
-        zb[side, OZ] = outer[1]
-        zb[side, OY] = outer[2]
-        zq[side, 0] = jnp.where(crosses, outer[1], own)
-        zq[side, 1] = jnp.where(crosses, 0.0, outer[2])
 
     def block_basis(i, edge):
         at = plane(i)
@@ -376,6 +339,73 @@
 
     for i in range(nx):
         block_basis(i, -1 if i == 0 else int(i == nx - 1))
+
+    for sx in sides:
+        @pl.when(has(sx, 0))
+        def _():
+            halo_copies(-sx)[1].wait_recv()
+    for sx, sz in diagonals:
+        @pl.when(has(sx, sz))
+        def _():
+            corner_copy(-sx, -sz).wait_recv()
+
+    for side in (0, 1):
+        k1 = kx[plane(1 if side == 0 else nx + 2), :]
+        k2 = kx[plane(0 if side == 0 else nx + 3), :]
+        toward = txf[plane(0 if side == 0 else nx), :]
+        inner = VERTICAL_RATIO * harmonic(k1, up(k1, 0))
+        tzm = jnp.where(sub == 0, VERTICAL_RATIO * harmonic(k1, crr[2 * side]), inner)
+        tzp = jnp.where(
+            sub == SUB - 1, VERTICAL_RATIO * harmonic(k1, crr[2 * side + 1]), down(inner, 0)
+        )
+        typ = y_face(k1)
+        tym = up(typ, 1)
+        crossing = (
+            toward,
+            only(cross_zm, tzm) + only(cross_zp, tzp),
+            only(cross_ym, tym) + only(cross_yp, typ),
+        )
+        _, own, outer = basis(
+            sk[plane(0 if side == 0 else nx + 1), :],
+            ((toward, harmonic(k1, k2)), (tzm, tzp), (tym, typ)),
+            crossing,
+        )
+        at = plane(0 if side == 0 else nx + 1)
+        own_s[at, :] = own
+        ox_s[plane(0 if side == 0 else 3), :] = outer[0]
+        oz_s[at, :] = outer[1]
+        oy_s[at, :] = outer[2]
+
+    wait_layers(1)
+    wait_layers(2)
+    wide_row = lax.broadcasted_iota(jnp.int32, (nx, ny), 0)
+    wide_lane = lax.broadcasted_iota(jnp.int32, (nx, ny), 1)
+    for side in (0, 1):
+        k1 = zr[side, 0]
+        k2 = zr[side, 1]
+        toward = tz_edge[side]
+        inner = harmonic(k1, up(k1, 0))
+        txm = jnp.where(wide_row == 0, harmonic(k1, crr[side]), inner)
+        txp = jnp.where(wide_row == nx - 1, harmonic(k1, crr[2 + side]), down(inner, 0))
+        typ = y_face(k1)
+        tym = up(typ, 1)
+        crosses = even if side == 0 else jnp.logical_not(even)
+        crossing = (
+            only(wide_row == 0, txm) + only(wide_row == nx - 1, txp),
+            toward * crosses.astype(jnp.float32),
+            only(wide_lane % EDGE == 0, tym) + only(wide_lane % EDGE == EDGE - 1, typ),
+        )
+        _, own, outer = basis(
+            zr[side, 2],
+            ((txm, txp), (toward, VERTICAL_RATIO * harmonic(k1, k2)), (tym, typ)),
+            crossing,
+        )
+        zb[side, OWN] = own
+        zb[side, OX] = outer[0]
+        zb[side, OZ] = outer[1]
+        zb[side, OY] = outer[2]
+        zq[side, 0] = jnp.where(crosses, outer[1], own)
+        zq[side, 1] = jnp.where(crosses, 0.0, outer[2])
 
     loads[2].wait()
     loads[3].wait()
@@ -516,14 +546,7 @@
             sums_of[PRODUCTS[n]] if n < len(PRODUCTS) else jnp.zeros((SUB, ny), jnp.float32)
         )
 
-    fine = lax.broadcasted_iota(jnp.int32, (ny, LANES), 0)
-    spot = lax.broadcasted_iota(jnp.int32, (ny, LANES), 1)
-    group = spot // cells
-    upper = group % 2
-    wanted = fine // EDGE + jnp.where(group >= 2, 2 * upper - 1, 0)
-    hit = (fine // HALF % 2 == upper) & (wanted == spot % cells) & (group < 4)
-    gather = jnp.where(hit, 1.0, 0.0).astype(jnp.bfloat16)
-    halves = split_dot(gather, acc[...], swap=True)
+    halves = split_dot(half_table[...], acc[...], swap=True)
     sums = halves.reshape(PADDED, SUB, LANES).sum(axis=1)
     stacked = jnp.concatenate(
         [sums] + [pltpu.roll(sums, LANES - g * cells, 1) for g in (1, 2, 3)], axis=0
@@ -674,7 +697,8 @@
     for sz in sides:
         @pl.when(has(0, sz))
         def _():
-            layer_copy(sz).wait_send()
+            for n in range(3):
+                layer_copy(sz, n).wait_send()
     for sx in sides:
         @pl.when(has(sx, 0))
         def _():
@@ -711,9 +735,9 @@
         f32(2, 2, nx, ny), f32(4, nx, ny),
         f32(*block), f32(*block), f32((nx + 1) * SUB, ny), f32(*block), f32(*block), f32(*block),
         f32(*wide), f32(*wide), f32(*wide), f32(4 * SUB, ny), f32(2, nx, ny), f32(2, 4, nx, ny),
-        pltpu.VMEM((3, nx, ny), jnp.int32), f32(PADDED * SUB, ny), f32(6, rows, LANES), f32(12, rows, LANES), f32(rows, LANES),
+        pltpu.VMEM((3, nx, ny), jnp.int32), pltpu.VMEM((ny, LANES), jnp.bfloat16), f32(PADDED * SUB, ny), f32(6, rows, LANES), f32(12, rows, LANES), f32(rows, LANES),
         f32(tiles * pairs, rows, LANES), f32(tiles * rows, LANES), f32(tiles, LANES),
-        dma((4,)), dma((2, 2)), dma((2, 2)), dma((2,)), dma((2,)), dma((4,)), dma((4,)),
+        dma((4,)), dma((2, 2)), dma((2, 2)), dma((2, 3)), dma((2, 3)), dma((4,)), dma((4,)),
         dma((12,)), dma((12,)), dma((tiles * pairs,)), dma((tiles * pairs,)),
     ]
     route = jnp.asarray(routing_table(), jnp.bfloat16)
@@ -724,7 +748,7 @@
         out_specs=pl.BlockSpec(memory_space=pltpu.VMEM),
         scratch_shapes=scratch,
         compiler_params=pltpu.CompilerParams(
-            collective_id=0, has_side_effects=True, vmem_limit_bytes=107 * 2**19
+            collective_id=0, has_side_effects=True, vmem_limit_bytes=215 * 2**18
         ),
     )(flat(classes), flat(well_mask), flat(source), route)
     return result.reshape(nx, nz, ny)

time: 23.8 us -> 24.5 us (1.029)
  local copies, waits for them, and re-layouts: 1.6 us -> 2.56 us
  Pallas kernels: 22 us -> 21.7 us
    unnamed x3, local copies, waits for them, and re-layouts: 1.6 us -> 2.56 us
    pallas_call x1, Pallas kernels: 22 us -> 21.7 us  [body(): pl.pallas_call(functools.partial(kernel, tiles, layers, nx, ny), out_shap...]
where the time goes in v4:
time: 24.5 us; the launch traced here: 24.3 us
  Pallas kernels  21.7 us (89%)
  local copies, waits for them, and re-layouts  2.56 us (10%)
    pallas_call x1, Pallas kernels, body(): pl.pallas_call(functools.partial(kernel, tiles, layers, nx, ny), out_shap...  21.7 us
    unnamed x3, local copies, waits for them, and re-layouts  2.56 us

profile of v4, /device:TPU:0, one launch (start us, length us, event | category | flops | bytes accessed | tf_op | source)
XLA Modules:
  0.0 24.3 jit_solution(2189944037104993660)
XLA Ops:
  0.0 0.0 copy-start
  0.0 0.9 %copy-done = bf16[2,96,160]{2,1,0:T(8,128)(2,1)S(1)} copy-done((bf16[2,96,160]{2,1,0:T(8,128)(2,1)S(1)}, bf16[2,96,160]{2,1,0:T(8,128)(2,1)}, u32[]{:S(2)}) %copy-start) | copy-done | bytes 61464
  0.9 21.7 %shard_map.46 = f32[128,512]{1,0:T(8,128)} custom-call(s32[128,512]{1,0:T(8,128)} %bitcast.5, s32[128,512]{1,0:T(8,128)} %bitcast.6, f32[128,512]{1,0:T(8,128)} %bitcast.7, bf16[2,96,160]{2,1,0:T(8,128)(2,1)S(1)} %copy-done), custom_call_target="tpu_custom_call" | custom-call | tf_op jit(solution)/shard_map/pallas_call | solution.py:744
  22.6 1.7 %copy.6 = f32[16,8,512]{2,1,0:T(8,128)} copy(f32[16,8,512]{2,1,0:T(8,128)} %bitcast.4) | data formatting | bytes 524288
Async XLA Ops:
  0.0 0.9 %copy-start = (bf16[2,96,160]{2,1,0:T(8,128)(2,1)S(1)}, bf16[2,96,160]{2,1,0:T(8,128)(2,1)}, u32[]{:S(2)}) copy-start(bf16[2,96,160]{2,1,0:T(8,128)(2,1)} %constant.2.clone.route_hbm) | copy-start | bytes 184324

commit v5 on v4

--- a/solution.py
+++ b/solution.py
@@ -66,6 +66,12 @@
         term = jnp.dot(*pair, preferred_element_type=jnp.float32)
         total = term if total is None else total + term
     return total
+
+
+def tree_sum(terms):
+    while len(terms) > 1:
+        terms = [sum(terms[n + 1 : n + 2], terms[n]) for n in range(0, len(terms), 2)]
+    return terms[0]
 
 
 def inverse_of(a):
@@ -598,9 +604,7 @@
                 ).wait_recv()
 
     terms = [part[2]] + [fold[slot] for slot in range(12)]
-    while len(terms) > 1:
-        terms = [sum(terms[n + 1 : n + 2], terms[n]) for n in range(0, len(terms), 2)]
-    gsend[...] = terms[0]
+    gsend[...] = tree_sum(terms)
 
     def gather_copy(k):
         other = lax.rem(tile * pairs + pair + k, tiles * pairs)
@@ -619,6 +623,27 @@
     spread = jnp.where(cell_at == parent, 1.0, 0.0).astype(jnp.bfloat16)
     beside_y = parent + 2 * (fine_at // HALF % 2) - 1
     spread_y = jnp.where(cell_at == beside_y, 1.0, 0.0).astype(jnp.bfloat16)
+
+    for sz in sides:
+        @pl.when(has(0, sz))
+        def _():
+            for n in range(3):
+                layer_copy(sz, n).wait_send()
+    for sx in sides:
+        @pl.when(has(sx, 0))
+        def _():
+            for copy in halo_copies(sx):
+                copy.wait_send()
+    for sx, sz in diagonals:
+        @pl.when(has(sx, sz))
+        def _():
+            corner_copy(sx, sz).wait_send()
+    for item in fold_list:
+        @pl.when(fold_valid(*item))
+        def _():
+            fold_copy(*item).wait_send()
+    for k in range(1, tiles * pairs):
+        gather_copy(k).wait_send()
 
     for k in range(1, tiles * pairs):
         frm = lax.rem(tile * pairs + pair + tiles * pairs - k, tiles * pairs)
@@ -658,11 +683,11 @@
     scale = COARSE_DAMPING / jnp.where(lane_t < span, forward[0], 1.0)
     coarse = rhs * scale
     for _ in range(SWEEPS - 1):
-        applied = forward[0] * coarse
+        terms = [forward[0] * coarse]
         for v in range(1, 14):
-            applied = applied + forward[v] * shifted(coarse, offsets[v])
-            applied = applied + backward[v] * shifted(coarse, [-d for d in offsets[v]])
-        coarse = coarse + (rhs - applied) * scale
+            terms.append(forward[v] * shifted(coarse, offsets[v]))
+            terms.append(backward[v] * shifted(coarse, [-d for d in offsets[v]]))
+        coarse = coarse + (rhs - tree_sum(terms)) * scale
     csc[...] = coarse
 
     def coarse_row(t, p):
@@ -694,27 +719,6 @@
             result = result + ox_s[plane(2), :] * wide[3 * SUB :, :]
         out_ref[plane(i), :] = result
 
-    for sz in sides:
-        @pl.when(has(0, sz))
-        def _():
-            for n in range(3):
-                layer_copy(sz, n).wait_send()
-    for sx in sides:
-        @pl.when(has(sx, 0))
-        def _():
-            for copy in halo_copies(sx):
-                copy.wait_send()
-    for sx, sz in diagonals:
-        @pl.when(has(sx, sz))
-        def _():
-            corner_copy(sx, sz).wait_send()
-    for item in fold_list:
-        @pl.when(fold_valid(*item))
-        def _():
-            fold_copy(*item).wait_send()
-    for k in range(1, tiles * pairs):
-        gather_copy(k).wait_send()
-
 
 def body(tiles, layers, classes, well_mask, source):
     nx, nz, ny = classes.shape
@@ -740,7 +744,7 @@
         dma((4,)), dma((2, 2)), dma((2, 2)), dma((2, 3)), dma((2, 3)), dma((4,)), dma((4,)),
         dma((12,)), dma((12,)), dma((tiles * pairs,)), dma((tiles * pairs,)),
     ]
-    route = jnp.asarray(routing_table(), jnp.bfloat16)
+    route = jnp.asarray(np.pad(routing_table(), ((0, 38), (0, 0), (0, 0))), jnp.bfloat16)
     result = pl.pallas_call(
         functools.partial(kernel, tiles, layers, nx, ny),
         out_shape=jax.ShapeDtypeStruct(block, jnp.float32),
@@ -748,7 +752,7 @@
         out_specs=pl.BlockSpec(memory_space=pltpu.VMEM),
         scratch_shapes=scratch,
         compiler_params=pltpu.CompilerParams(
-            collective_id=0, has_side_effects=True, vmem_limit_bytes=215 * 2**18
+            collective_id=0, has_side_effects=True, vmem_limit_bytes=107 * 2**19
         ),
     )(flat(classes), flat(well_mask), flat(source), route)
     return result.reshape(nx, nz, ny)

time: 24.5 us -> 21.8 us (0.89)
  local copies, waits for them, and re-layouts: 2.56 us -> 0.71 us
  Pallas kernels: 21.7 us -> 20.9 us
    unnamed x3 -> x1, local copies, waits for them, and re-layouts: 2.56 us -> 0.71 us
    pallas_call x1, Pallas kernels: 21.7 us -> 20.9 us  [body(): pl.pallas_call(functools.partial(kernel, tiles, layers, nx, ny), out_shap...]
where the time goes in v5:
time: 21.8 us; the launch traced here: 21.6 us
  Pallas kernels  20.9 us (96%)
  local copies, waits for them, and re-layouts  0.71 us (3%)
    pallas_call x1, Pallas kernels, body(): pl.pallas_call(functools.partial(kernel, tiles, layers, nx, ny), out_shap...  20.9 us
    unnamed x1, local copies, waits for them, and re-layouts  0.71 us

profile of v5, /device:TPU:0, one launch (start us, length us, event | category | flops | bytes accessed | tf_op | source)
XLA Modules:
  0.0 21.6 jit_solution(11324376669947758993)
XLA Ops:
  0.0 20.9 %shard_map.46 = f32[128,512]{1,0:T(8,128)S(1)} custom-call(s32[128,512]{1,0:T(8,128)} %bitcast.5, s32[128,512]{1,0:T(8,128)} %bitcast.6, f32[128,512]{1,0:T(8,128)} %bitcast.7, bf16[40,96,160]{2,1,0:T(8,128)(2,1)} %constant.2.clone.route_hbm), custom_call_target="tpu_custom_call" | custom-call | tf_op jit(solution)/shard_map/pallas_call | solution.py:748
  20.9 0.7 %copy.6 = f32[16,8,512]{2,1,0:T(8,128)} copy(f32[16,8,512]{2,1,0:T(8,128)S(1)} %bitcast.4) | data formatting | bytes 524288

commit v6 on v5

--- a/solution.py
+++ b/solution.py
@@ -147,22 +147,29 @@
     loads[2].start()
     loads[3].start()
 
-    for i in (0, 1, nx - 2, nx - 1):
-        k = perm_of(cls[plane(i), :])
-        kx[plane(i + 2), :] = k
-        if i in (0, nx - 1):
-            sk[plane(i + 1), :] = sink_of(well[plane(i), :], k)
-    for side, (z1, z2) in enumerate(((0, 1), (SUB - 1, SUB - 2))):
+    ends = ((0, 1), (SUB - 1, SUB - 2))
+    for side, (z1, z2) in enumerate(ends):
         for i in range(nx):
-            zi[0, pl.ds(i, 1), :] = cls[pl.ds(i * SUB + z1, 1), :]
-            zi[1, pl.ds(i, 1), :] = cls[pl.ds(i * SUB + z2, 1), :]
-            zi[2, pl.ds(i, 1), :] = well[pl.ds(i * SUB + z1, 1), :]
-        k = perm_of(zi[0])
+            zi[side, pl.ds(i, 1), :] = cls[pl.ds(i * SUB + z1, 1), :]
+        k = perm_of(zi[side])
         zs[side, 0] = k
-        zs[side, 1] = perm_of(zi[1])
-        zs[side, 2] = sink_of(zi[2], k)
         crs[0 + side] = k[0:1, :]
         crs[2 + side] = k[nx - 1 : nx, :]
+
+    def pack_planes():
+        for i in (0, 1, nx - 2, nx - 1):
+            k = perm_of(cls[plane(i), :])
+            kx[plane(i + 2), :] = k
+            if i in (0, nx - 1):
+                sk[plane(i + 1), :] = sink_of(well[plane(i), :], k)
+
+    def pack_rows():
+        for side, (z1, z2) in enumerate(ends):
+            for i in range(nx):
+                zi[2 + side, pl.ds(i, 1), :] = cls[pl.ds(i * SUB + z2, 1), :]
+                zi[4 + side, pl.ds(i, 1), :] = well[pl.ds(i * SUB + z1, 1), :]
+            zs[side, 1] = perm_of(zi[2 + side])
+            zs[side, 2] = sink_of(zi[4 + side], zs[side, 0])
 
     pl.semaphore_wait(barrier, tiles * layers - 1)
 
@@ -214,6 +221,7 @@
         @pl.when(jnp.logical_not(has(0, sz)))
         def _():
             zr[0 if sz < 0 else 1] = jnp.zeros(zr.shape[1:], jnp.float32)
+    pack_planes()
     for sx in sides:
         @pl.when(has(sx, 0))
         def _():
@@ -233,6 +241,7 @@
         @pl.when(jnp.logical_not(has(sx, sz)))
         def _():
             crr[2 * (0 if sx < 0 else 1) + (0 if sz < 0 else 1)] = jnp.zeros((1, ny), jnp.float32)
+    pack_rows()
     for sz in sides:
         @pl.when(has(0, sz))
         def _():
@@ -547,13 +556,28 @@
     add_rows((OX, FULL_OFFSETS[3], -1), only(first, ox * qzy))
     ox_in = only(first, ox_s[pl.ds(SUB + z2, 1), :])
     add_rows((OX, FULL_OFFSETS[2], -1), only(first, ox * qz) + ox_in * qz_in)
-    for n in range(PADDED):
-        acc[plane(n), :] = (
-            sums_of[PRODUCTS[n]] if n < len(PRODUCTS) else jnp.zeros((SUB, ny), jnp.float32)
-        )
-
-    halves = split_dot(half_table[...], acc[...], swap=True)
-    sums = halves.reshape(PADDED, SUB, LANES).sum(axis=1)
+    def merge(a, b, distance):
+        lower = sub // distance % 2 == 0
+        if 2 * distance == SUB:
+            return jnp.where(lower, a, b) + pltpu.roll(jnp.where(lower, b, a), distance, 0)
+        return jnp.where(
+            lower, a + pltpu.roll(a, SUB - distance, 0), b + pltpu.roll(b, distance, 0)
+        )
+
+    nothing = jnp.zeros((SUB, ny), jnp.float32)
+    for first_row in range(0, PADDED, SUB):
+        group_of = [
+            sums_of[PRODUCTS[n]] if n < len(PRODUCTS) else nothing
+            for n in range(first_row, first_row + SUB)
+        ]
+        while len(group_of) > 1:
+            distance = len(group_of) // 2
+            group_of = [
+                merge(group_of[j], group_of[j + distance], distance) for j in range(distance)
+            ]
+        acc[pl.ds(first_row, SUB), :] = group_of[0]
+
+    sums = split_dot(half_table[...], acc[...], swap=True)
     stacked = jnp.concatenate(
         [sums] + [pltpu.roll(sums, LANES - g * cells, 1) for g in (1, 2, 3)], axis=0
     )
@@ -613,7 +637,10 @@
             device_id=(other // pairs, 2 * (other % pairs) + parity), device_id_type=MESH,
         )
 
-    for k in range(1, tiles * pairs):
+    far_first = sorted(
+        range(1, tiles * pairs), key=lambda k: (k % pairs == 0, abs(k - tiles * pairs // 2))
+    )
+    for k in far_first:
         gather_copy(k).start()
     gath[tile * pairs + pair] = gsend[...]
 
@@ -739,7 +766,7 @@
         f32(2, 2, nx, ny), f32(4, nx, ny),
         f32(*block), f32(*block), f32((nx + 1) * SUB, ny), f32(*block), f32(*block), f32(*block),
         f32(*wide), f32(*wide), f32(*wide), f32(4 * SUB, ny), f32(2, nx, ny), f32(2, 4, nx, ny),
-        pltpu.VMEM((3, nx, ny), jnp.int32), pltpu.VMEM((ny, LANES), jnp.bfloat16), f32(PADDED * SUB, ny), f32(6, rows, LANES), f32(12, rows, LANES), f32(rows, LANES),
+        pltpu.VMEM((6, nx, ny), jnp.int32), pltpu.VMEM((ny, LANES), jnp.bfloat16), f32(PADDED, ny), f32(6, rows, LANES), f32(12, rows, LANES), f32(rows, LANES),
         f32(tiles * pairs, rows, LANES), f32(tiles * rows, LANES), f32(tiles, LANES),
         dma((4,)), dma((2, 2)), dma((2, 2)), dma((2, 3)), dma((2, 3)), dma((4,)), dma((4,)),
         dma((12,)), dma((12,)), dma((tiles * pairs,)), dma((tiles * pairs,)),

time: 21.8 us -> 21.7 us (level)
  no operation moved by 1% of the time
where the time goes in v6:
time: 21.7 us; the launch traced here: 21.5 us
  Pallas kernels  20.8 us (96%)
  local copies, waits for them, and re-layouts  0.71 us (3%)
    pallas_call x1, Pallas kernels, body(): pl.pallas_call(functools.partial(kernel, tiles, layers, nx, ny), out_shap...  20.8 us
    unnamed x1, local copies, waits for them, and re-layouts  0.71 us

profile of v6, /device:TPU:0, one launch (start us, length us, event | category | flops | bytes accessed | tf_op | source)
XLA Modules:
  0.0 21.5 jit_solution(12131468326228099765)
XLA Ops:
  0.0 20.8 %shard_map.46 = f32[128,512]{1,0:T(8,128)S(1)} custom-call(s32[128,512]{1,0:T(8,128)} %bitcast.5, s32[128,512]{1,0:T(8,128)} %bitcast.6, f32[128,512]{1,0:T(8,128)} %bitcast.7, bf16[40,96,160]{2,1,0:T(8,128)(2,1)} %constant.2.clone.route_hbm), custom_call_target="tpu_custom_call" | custom-call | tf_op jit(solution)/shard_map/pallas_call | solution.py:775
  20.8 0.7 %copy.6 = f32[16,8,512]{2,1,0:T(8,128)} copy(f32[16,8,512]{2,1,0:T(8,128)S(1)} %bitcast.4) | data formatting | bytes 524288

commit v7 on v6

--- a/solution.py
+++ b/solution.py
@@ -97,7 +97,7 @@
     tiles, layers, nx, ny,
     cls_hbm, well_hbm, src_hbm, route_hbm, out_ref,
     cls, well, src, route,
-    kx, sk, zs, zr, crs, crr, zq, ze,
+    kx, sk, zs, zr, crs, crr, zq, zw, ze,
     typ_s, tzi_s, txf, tzm_s, tzp_s, d_s, own_s, oy_s, oz_s, ox_s, tz_edge, zb,
     zi, half_table, acc, part, fold, gsend, gath, gsum, csc,
     in_sem, x_send, x_recv, z_send, z_recv, c_send, c_recv, f_send, f_recv, g_send, g_recv,
@@ -391,37 +391,6 @@
         oz_s[at, :] = outer[1]
         oy_s[at, :] = outer[2]
 
-    wait_layers(1)
-    wait_layers(2)
-    wide_row = lax.broadcasted_iota(jnp.int32, (nx, ny), 0)
-    wide_lane = lax.broadcasted_iota(jnp.int32, (nx, ny), 1)
-    for side in (0, 1):
-        k1 = zr[side, 0]
-        k2 = zr[side, 1]
-        toward = tz_edge[side]
-        inner = harmonic(k1, up(k1, 0))
-        txm = jnp.where(wide_row == 0, harmonic(k1, crr[side]), inner)
-        txp = jnp.where(wide_row == nx - 1, harmonic(k1, crr[2 + side]), down(inner, 0))
-        typ = y_face(k1)
-        tym = up(typ, 1)
-        crosses = even if side == 0 else jnp.logical_not(even)
-        crossing = (
-            only(wide_row == 0, txm) + only(wide_row == nx - 1, txp),
-            toward * crosses.astype(jnp.float32),
-            only(wide_lane % EDGE == 0, tym) + only(wide_lane % EDGE == EDGE - 1, typ),
-        )
-        _, own, outer = basis(
-            zr[side, 2],
-            ((txm, txp), (toward, VERTICAL_RATIO * harmonic(k1, k2)), (tym, typ)),
-            crossing,
-        )
-        zb[side, OWN] = own
-        zb[side, OX] = outer[0]
-        zb[side, OZ] = outer[1]
-        zb[side, OY] = outer[2]
-        zq[side, 0] = jnp.where(crosses, outer[1], own)
-        zq[side, 1] = jnp.where(crosses, 0.0, outer[2])
-
     loads[2].wait()
     loads[3].wait()
 
@@ -431,7 +400,7 @@
         sums_of[product] = sums_of[product] + term if product in sums_of else term
 
     def products(i, edge):
-        at, mid, after, row = plane(i), plane(i + 1), plane(i + 2), pl.ds(i, 1)
+        at, mid, after = plane(i), plane(i + 1), plane(i + 2)
         diagonal, tzm, tzp, typ = d_s[at, :], tzm_s[at, :], tzp_s[at, :], typ_s[at, :]
         tym = up(typ, 1)
         txm, txp = txf[at, :], txf[mid, :]
@@ -440,14 +409,14 @@
         swap_m, swap_p = jnp.where(cross_yp, oy, own), jnp.where(cross_ym, oy, own)
         keep_m, keep_p = jnp.where(cross_yp, own, oy), jnp.where(cross_ym, own, oy)
 
-        def z_pair(a, kind):
+        def z_pair(a):
             return (
-                jnp.where(sub == 0, zq[0, kind, row, :], up(a, 0)),
-                jnp.where(sub == SUB - 1, zq[1, kind, row, :], down(a, 0)),
+                only(sub != 0, up(a, 0)),
+                only(sub != SUB - 1, down(a, 0)),
             )
 
-        own_zm, own_zp = z_pair(own, 0)
-        oy_zm, oy_zp = z_pair(oy, 1)
+        own_zm, own_zp = z_pair(own)
+        oy_zm, oy_zp = z_pair(oy)
         before_own = ox_s[plane(0), :] if edge < 0 else own_s[at, :]
         after_own = ox_s[plane(3), :] if edge > 0 else own_s[after, :]
         q0 = (
@@ -466,16 +435,21 @@
         for kind, weight in ((OWN, own), (OY, oy)):
             for offset, field in fields:
                 add((kind, offset, 0), weight * field)
-        if not edge:
-            return
-        ox = ox_s[plane(1 if edge < 0 else 2), :]
         if edge < 0:
+            ox = ox_s[plane(1), :]
             for offset, field in fields:
                 add((OX, offset, -1), ox * field)
-            across, t_across = plane(0), txm
-        else:
-            add((OX, None, 1), ox * source)
-            across, t_across = plane(nx + 1), txp
+        if edge > 0:
+            add((OX, None, 1), ox_s[plane(2), :] * source)
+
+    def edge_products(i, edge):
+        at, mid, row = plane(i), plane(i + 1), pl.ds(i, 1)
+        diagonal, tzm, tzp, typ = d_s[at, :], tzm_s[at, :], tzp_s[at, :], typ_s[at, :]
+        tym = up(typ, 1)
+        txm, txp = txf[at, :], txf[mid, :]
+        own, oy = own_s[mid, :], oy_s[mid, :]
+        ox = ox_s[plane(1 if edge < 0 else 2), :]
+        across, t_across = (plane(0), txm) if edge < 0 else (plane(nx + 1), txp)
         tymc, typc = only(cross_ym, tym), only(cross_yp, typ)
         tzmc, tzpc = only(cross_zm, tzm), only(cross_zp, tzp)
         ox_ym, ox_yp = up(ox, 1), down(ox, 1)
@@ -500,12 +474,18 @@
     for i in range(nx):
         products(i, -1 if i == 0 else int(i == nx - 1))
 
+    wide_row = lax.broadcasted_iota(jnp.int32, (nx, ny), 0)
+    wide_lane = lax.broadcasted_iota(jnp.int32, (nx, ny), 1)
     z1 = parity * (SUB - 1)
     z2 = 1 + parity * (SUB - 3)
     for i in range(nx):
         ze[1, pl.ds(i, 1), :] = own_s[pl.ds((i + 1) * SUB + z2, 1), :]
         ze[2, pl.ds(i, 1), :] = oy_s[pl.ds((i + 1) * SUB + z2, 1), :]
         ze[3, pl.ds(i, 1), :] = src[pl.ds(i * SUB + z1, 1), :]
+        for side in (0, 1):
+            at = pl.ds((i + 1) * SUB + side * (SUB - 1), 1)
+            zw[side, 0, pl.ds(i, 1), :] = own_s[at, :]
+            zw[side, 1, pl.ds(i, 1), :] = oy_s[at, :]
     first, last = wide_row == 0, wide_row == nx - 1
     wide_ym, wide_yp = wide_lane % EDGE == 0, wide_lane % EDGE == EDGE - 1
     k1 = zs[parity, 0]
@@ -524,6 +504,52 @@
     )
     ze[0] = oz
     txmn, txpn, tymn, typn = txm - txmc, txp - txpc, tym - tymc, typ - typc
+    def rows_beside():
+        wait_layers(1)
+        wait_layers(2)
+        for side in (0, 1):
+            k1 = zr[side, 0]
+            k2 = zr[side, 1]
+            toward = tz_edge[side]
+            inner = harmonic(k1, up(k1, 0))
+            txm = jnp.where(wide_row == 0, harmonic(k1, crr[side]), inner)
+            txp = jnp.where(wide_row == nx - 1, harmonic(k1, crr[2 + side]), down(inner, 0))
+            typ = y_face(k1)
+            tym = up(typ, 1)
+            crosses = even if side == 0 else jnp.logical_not(even)
+            crossing = (
+                only(wide_row == 0, txm) + only(wide_row == nx - 1, txp),
+                toward * crosses.astype(jnp.float32),
+                only(wide_lane % EDGE == 0, tym) + only(wide_lane % EDGE == EDGE - 1, typ),
+            )
+            _, own, outer = basis(
+                zr[side, 2],
+                ((txm, txp), (toward, VERTICAL_RATIO * harmonic(k1, k2)), (tym, typ)),
+                crossing,
+            )
+            zb[side, OWN] = own
+            zb[side, OX] = outer[0]
+            zb[side, OZ] = outer[1]
+            zb[side, OY] = outer[2]
+            zq[side, 0] = jnp.where(crosses, outer[1], own)
+            zq[side, 1] = jnp.where(crosses, 0.0, outer[2])
+
+    rows_beside()
+    def add_rows(product, term):
+        add(product, term[:SUB, :] + term[SUB:, :])
+
+    for i, edge in ((0, -1), (nx - 1, 1)):
+        edge_products(i, edge)
+    for side in (0, 1):
+        weights = (
+            (OWN, 0, zw[side, 0]), (OY, 0, zw[side, 1]),
+            (OX, -1, only(first, ox_s[pl.ds(SUB + side * (SUB - 1), 1), :])),
+        )
+        for n, offset in enumerate(FULL_OFFSETS[:2]):
+            field = -tz_edge[side] * zq[side, n]
+            for kind, at_side, weight in weights:
+                add_rows((kind, offset, at_side), weight * field)
+
     own_in, oy_in, source = ze[1], ze[2], ze[3]
     ox_before, ox_after = ox_s[pl.ds(z1, 1), :], ox_s[pl.ds(3 * SUB + z1, 1), :]
     oz_ym, oz_yp = up(oz, 1), down(oz, 1)
@@ -543,9 +569,6 @@
     )
     qz_in = -t_in * oz
     qzy = -(tymc * oz_ym + typc * oz_yp + t_out * zb[parity, OY])
-
-    def add_rows(product, term):
-        add(product, term[:SUB, :] + term[SUB:, :])
 
     for offset, field in zip(FULL_OFFSETS, (q0, qy, qz, qzy, source)):
         add_rows((OZ, offset, 0), oz * field)
@@ -763,7 +786,7 @@
         pltpu.VMEM((6 * VALUES, 4 * PADDED), jnp.bfloat16),
         f32((nx + 4) * SUB, ny), f32(*wide), f32(2, 3, nx, ny), f32(2, 3, nx, ny),
         f32(4, 1, ny), f32(4, 1, ny),
-        f32(2, 2, nx, ny), f32(4, nx, ny),
+        f32(2, 2, nx, ny), f32(2, 2, nx, ny), f32(4, nx, ny),
         f32(*block), f32(*block), f32((nx + 1) * SUB, ny), f32(*block), f32(*block), f32(*block),
         f32(*wide), f32(*wide), f32(*wide), f32(4 * SUB, ny), f32(2, nx, ny), f32(2, 4, nx, ny),
         pltpu.VMEM((6, nx, ny), jnp.int32), pltpu.VMEM((ny, LANES), jnp.bfloat16), f32(PADDED, ny), f32(6, rows, LANES), f32(12, rows, LANES), f32(rows, LANES),

time: 21.7 us -> 21.2 us (0.977)
  Pallas kernels: 20.8 us -> 20.4 us
    pallas_call x1, Pallas kernels: 20.8 us -> 20.4 us  [body(): pl.pallas_call(functools.partial(kernel, tiles, layers, nx, ny), out_shap...]
where the time goes in v7:
time: 21.2 us; the launch traced here: 21.1 us
  Pallas kernels  20.4 us (96%)
  local copies, waits for them, and re-layouts  0.71 us (3%)
    pallas_call x1, Pallas kernels, body(): pl.pallas_call(functools.partial(kernel, tiles, layers, nx, ny), out_shap...  20.4 us
    unnamed x1, local copies, waits for them, and re-layouts  0.71 us

profile of v7, /device:TPU:0, one launch (start us, length us, event | category | flops | bytes accessed | tf_op | source)
XLA Modules:
  0.0 21.1 jit_solution(9029004096036527848)
XLA Ops:
  0.0 20.4 %shard_map.46 = f32[128,512]{1,0:T(8,128)S(1)} custom-call(s32[128,512]{1,0:T(8,128)} %bitcast.5, s32[128,512]{1,0:T(8,128)} %bitcast.6, f32[128,512]{1,0:T(8,128)} %bitcast.7, bf16[40,96,160]{2,1,0:T(8,128)(2,1)} %constant.2.clone.route_hbm), custom_call_target="tpu_custom_call" | custom-call | tf_op jit(solution)/shard_map/pallas_call | solution.py:798
  20.4 0.7 %copy.6 = f32[16,8,512]{2,1,0:T(8,128)} copy(f32[16,8,512]{2,1,0:T(8,128)S(1)} %bitcast.4) | data formatting | bytes 524288

commit v8 on v7

--- a/solution.py
+++ b/solution.py
@@ -612,10 +612,12 @@
     near_pair = jnp.clip(beside_pair, 0, pairs - 1)
     for target in range(6):
         block = routed[target * VALUES : (target + 1) * VALUES, :]
-        if rows < VALUES:
-            block = block[:rows, :] + pltpu.roll(block[rows:, :], span, 1)
-        to_pair = near_pair if target % 2 else pair
-        part[target] = pltpu.roll(block, to_pair * cells, 1)
+        part[target] = tree_sum(
+            [
+                pltpu.roll(block[g * rows : (g + 1) * rows, :], g * cells, 1) if g else block[:rows, :]
+                for g in range(VALUES // rows)
+            ]
+        )
 
     def fold_copy(sx, beside, which):
         to_pair = beside_pair if beside else pair
@@ -702,18 +704,19 @@
             device_id=(tile, layer), device_id_type=MESH,
         ).wait_recv()
 
-    for t in range(tiles):
-        total = gath[t * pairs]
-        for p in range(1, pairs):
-            total = total + gath[t * pairs + p]
-        gsum[pl.ds(t * rows, rows), :] = total
+    for p in range(pairs):
+        for t in range(tiles):
+            gsum[pl.ds((p * tiles + t) * rows, rows), :] = gath[t * pairs + p]
     lane_t = lax.broadcasted_iota(jnp.int32, (tiles, LANES), 1)
 
     def value(v):
-        a = gsum[pl.ds(v % rows, tiles, stride=rows), :]
-        if v >= rows:
-            a = pltpu.roll(a, LANES - span, 1)
-        return only(lane_t < span, a)
+        total = None
+        for p in range(pairs):
+            a = gsum[pl.ds(p * tiles * rows + v % rows, tiles, stride=rows), :]
+            shift = (p - v // rows) * cells % LANES
+            a = only(lane_t // cells == p, pltpu.roll(a, shift, 1) if shift else a)
+            total = a if total is None else total + a
+        return total
 
     def shifted(a, offset):
         ox, oz, oy = offset
@@ -774,8 +777,8 @@
     nx, nz, ny = classes.shape
     assert nx == EDGE and nz == HALF == SUB and layers % 2 == 0
     cells, pairs = ny // EDGE, layers // 2
-    assert 4 * cells <= LANES and pairs * cells <= LANES
-    rows = VALUES // 2 if 2 * pairs * cells <= LANES else VALUES
+    assert 4 * cells == LANES and pairs * cells <= LANES
+    rows = VALUES * cells // LANES
     flat = lambda a: a.reshape(nx * nz, ny)
     f32 = lambda *shape: pltpu.VMEM(shape, jnp.float32)
     dma = pltpu.SemaphoreType.DMA
@@ -790,7 +793,7 @@
         f32(*block), f32(*block), f32((nx + 1) * SUB, ny), f32(*block), f32(*block), f32(*block),
         f32(*wide), f32(*wide), f32(*wide), f32(4 * SUB, ny), f32(2, nx, ny), f32(2, 4, nx, ny),
         pltpu.VMEM((6, nx, ny), jnp.int32), pltpu.VMEM((ny, LANES), jnp.bfloat16), f32(PADDED, ny), f32(6, rows, LANES), f32(12, rows, LANES), f32(rows, LANES),
-        f32(tiles * pairs, rows, LANES), f32(tiles * rows, LANES), f32(tiles, LANES),
+        f32(tiles * pairs, rows, LANES), f32(pairs * tiles * rows, LANES), f32(tiles, LANES),
         dma((4,)), dma((2, 2)), dma((2, 2)), dma((2, 3)), dma((2, 3)), dma((4,)), dma((4,)),
         dma((12,)), dma((12,)), dma((tiles * pairs,)), dma((tiles * pairs,)),
     ]

time: 21.2 us -> 21 us (level)
  no operation moved by 1% of the time
where the time goes in v8:
time: 21 us; the launch traced here: 20.9 us
  Pallas kernels  20.2 us (96%)
  local copies, waits for them, and re-layouts  0.71 us (3%)
    pallas_call x1, Pallas kernels, body(): pl.pallas_call(functools.partial(kernel, tiles, layers, nx, ny), out_shap...  20.2 us
    unnamed x1, local copies, waits for them, and re-layouts  0.71 us

profile of v8, /device:TPU:0, one launch (start us, length us, event | category | flops | bytes accessed | tf_op | source)
XLA Modules:
  0.0 20.9 jit_solution(5046915236696414131)
XLA Ops:
  0.0 20.2 %shard_map.46 = f32[128,512]{1,0:T(8,128)S(1)} custom-call(s32[128,512]{1,0:T(8,128)} %bitcast.5, s32[128,512]{1,0:T(8,128)} %bitcast.6, f32[128,512]{1,0:T(8,128)} %bitcast.7, bf16[40,96,160]{2,1,0:T(8,128)(2,1)} %constant.2.clone.route_hbm), custom_call_target="tpu_custom_call" | custom-call | tf_op jit(solution)/shard_map/pallas_call | solution.py:801
  20.2 0.7 %copy.6 = f32[16,8,512]{2,1,0:T(8,128)} copy(f32[16,8,512]{2,1,0:T(8,128)S(1)} %bitcast.4) | data formatting | bytes 524288

commit v9 on v8

--- a/solution.py
+++ b/solution.py
@@ -143,9 +143,6 @@
                 fold[(dt + 1) * 4 + role] = jnp.zeros(fold.shape[1:], jnp.float32)
 
     loads[0].wait()
-    loads[1].wait()
-    loads[2].start()
-    loads[3].start()
 
     ends = ((0, 1), (SUB - 1, SUB - 2))
     for side, (z1, z2) in enumerate(ends):
@@ -160,8 +157,13 @@
         for i in (0, 1, nx - 2, nx - 1):
             k = perm_of(cls[plane(i), :])
             kx[plane(i + 2), :] = k
-            if i in (0, nx - 1):
-                sk[plane(i + 1), :] = sink_of(well[plane(i), :], k)
+
+    def pack_sinks():
+        loads[1].wait()
+        loads[2].start()
+        loads[3].start()
+        for i in (0, nx - 1):
+            sk[plane(i + 1), :] = sink_of(well[plane(i), :], kx[plane(i + 2), :])
 
     def pack_rows():
         for side, (z1, z2) in enumerate(ends):
@@ -225,8 +227,7 @@
     for sx in sides:
         @pl.when(has(sx, 0))
         def _():
-            for copy in halo_copies(sx):
-                copy.start()
+            halo_copies(sx)[0].start()
 
         @pl.when(jnp.logical_not(has(sx, 0)))
         def _():
@@ -241,6 +242,12 @@
         @pl.when(jnp.logical_not(has(sx, sz)))
         def _():
             crr[2 * (0 if sx < 0 else 1) + (0 if sz < 0 else 1)] = jnp.zeros((1, ny), jnp.float32)
+    pack_sinks()
+    for sx in sides:
+        @pl.when(has(sx, 0))
+        def _():
+            halo_copies(sx)[1].start()
+
     pack_rows()
     for sz in sides:
         @pl.when(has(0, sz))

time: 21 us -> 21 us (level)
  no operation moved by 1% of the time
where the time goes in v9:
time: 21 us; the launch traced here: 20.9 us
  Pallas kernels  20.2 us (96%)
  local copies, waits for them, and re-layouts  0.71 us (3%)
    pallas_call x1, Pallas kernels, body(): pl.pallas_call(functools.partial(kernel, tiles, layers, nx, ny), out_shap...  20.2 us
    unnamed x1, local copies, waits for them, and re-layouts  0.71 us

profile of v9, /device:TPU:0, one launch (start us, length us, event | category | flops | bytes accessed | tf_op | source)
XLA Modules:
  0.0 20.9 jit_solution(17161640911547470283)
XLA Ops:
  0.0 20.2 %shard_map.46 = f32[128,512]{1,0:T(8,128)S(1)} custom-call(s32[128,512]{1,0:T(8,128)} %bitcast.5, s32[128,512]{1,0:T(8,128)} %bitcast.6, f32[128,512]{1,0:T(8,128)} %bitcast.7, bf16[40,96,160]{2,1,0:T(8,128)(2,1)} %constant.2.clone.route_hbm), custom_call_target="tpu_custom_call" | custom-call | tf_op jit(solution)/shard_map/pallas_call | solution.py:808
  20.2 0.7 %copy.6 = f32[16,8,512]{2,1,0:T(8,128)} copy(f32[16,8,512]{2,1,0:T(8,128)S(1)} %bitcast.4) | data formatting | bytes 524288
